TPU v7x, 32 devices: a whole 2x2x4 slice. The times are simulated.
32 devices in a mesh: gr: 4 (over z), gc: 8 (over y, x, core).
Axes of the slice: x: 2, y: 2, z: 4, core: 2. Of those that a mesh axis runs over, the one named last changes fastest.
Arguments:
- embeddings: bfloat16 [8192, 768], P(('gr', 'gc'))
- cluster_ids: int32 [8192], P(('gr', 'gc')), may hold values from 0 to 3, as said below
Outputs:
- neighbour_sum: float32 [8192, 768], P(('gr', 'gc'))
- density: float32 [8192], P(('gr', 'gc'))
Inputs may be any that keep to these rules, and one draw needn't show every extreme that they name: `cluster_ids`: each device's 256 rows hold exactly 64 rows of every cluster.
All inputs are finite; a program needn't handle non-finite values.
Results may differ from a plain program's by a relative error of at most 0.0017.
Values may be sent and summed in bfloat16 or wider, within the bound.
No kernel may reach another device: no remote copies, remote signals or barrier semaphores. Data moves between devices by JAX's collectives and lax.ppermute only.
A program may use at most 128 MiB of HBM per device.

v0:
```python
import functools
import math

import jax
import jax.numpy as jnp
from jax import lax
from jax.experimental import pallas as pl
from jax.experimental.pallas import tpu as pltpu
from jax.sharding import PartitionSpec as P

beta_scale = 16.0
LANES = 128
VMEM = pl.BlockSpec(memory_space=pltpu.VMEM)
SMEM = pl.BlockSpec(memory_space=pltpu.SMEM)
GRANT = pltpu.CompilerParams(vmem_limit_bytes=40 * 1024 * 1024)


def placement(own, ids, groups):
    count = ids.shape[1]
    first = lax.broadcasted_iota(jnp.int32, (count, count), 0)
    second = lax.broadcasted_iota(jnp.int32, (count, count), 1)
    turned = jnp.sum(jnp.where(first == second, ids, 0), axis=1, keepdims=True)
    earlier = jnp.where((turned == ids) & (first < second), 1, 0)
    rank = jnp.sum(earlier, axis=0, keepdims=True)
    slot = (ids ^ own) * (count // groups) + rank
    return jnp.where(first == slot, 1.0, 0.0).astype(jnp.bfloat16)


def sort_kernel(own_ref, ids_ref, rows_ref, *out_refs):
    groups = len(out_refs)
    chosen = placement(own_ref[0], ids_ref[...], groups)
    ordered = jnp.dot(chosen, rows_ref[...], preferred_element_type=jnp.float32)
    ordered = ordered.astype(jnp.bfloat16)
    size = ordered.shape[0] // groups
    for k, out_ref in enumerate(out_refs):
        out_ref[...] = ordered[k * size : (k + 1) * size, :]


def inverse_norms(rows):
    wide = rows.astype(jnp.float32)
    return lax.rsqrt(jnp.sum(wide * wide, axis=1, keepdims=True) + 1e-06)


def add_columns(rows, col_refs, total, dens):
    count = rows.shape[0]
    scale = inverse_norms(rows) * (beta_scale * math.log2(math.e))
    for col_ref in col_refs:
        cols = col_ref[...]
        size = cols.shape[0]
        first = lax.broadcasted_iota(jnp.int32, (size, size), 0)
        second = lax.broadcasted_iota(jnp.int32, (size, size), 1)
        col_inv = jnp.sum(
            jnp.where(first == second, inverse_norms(cols), 0.0), axis=0, keepdims=True
        )
        raw = lax.dot_general(
            rows, cols, (((1,), (1,)), ((), ())), preferred_element_type=jnp.float32
        )
        weight = jnp.exp2(raw * scale * col_inv - beta_scale * math.log2(math.e))
        for start in range(0, size, LANES):
            dens += weight[:, start : start + LANES]
        coef = (weight * col_inv).astype(jnp.bfloat16)
        total += jnp.dot(coef, cols, preferred_element_type=jnp.float32)
    return total, dens


def first_kernel(rows_ref, *refs):
    col_refs, (total_ref, dens_ref) = refs[:-2], refs[-2:]
    total = jnp.zeros(total_ref.shape, jnp.float32)
    dens = jnp.zeros(dens_ref.shape, jnp.float32)
    total, dens = add_columns(rows_ref[...], col_refs, total, dens)
    total_ref[...] = total
    dens_ref[...] = dens


def last_kernel(n_out, rows_ref, total_ref, dens_ref, *refs):
    col_refs, out_refs = refs[:-n_out], refs[-n_out:]
    count, width = rows_ref.shape
    total, dens = add_columns(rows_ref[...], col_refs, total_ref[...], dens_ref[...])
    dens = jnp.broadcast_to(jnp.sum(dens, axis=1, keepdims=True), dens.shape)
    size = count // n_out
    for k, out_ref in enumerate(out_refs):
        out_ref[:, :width] = total[k * size : (k + 1) * size, :]
        out_ref[:, width:] = dens[k * size : (k + 1) * size, :]


def restore_kernel(own_ref, ids_ref, *refs):
    part_refs, (total_ref, dens_ref) = refs[:-2], refs[-2:]
    width = total_ref.shape[1]
    chosen = placement(own_ref[0], ids_ref[...], len(part_refs))
    rest = jnp.concatenate([ref[...] for ref in part_refs], axis=0)
    back = jnp.zeros(rest.shape, jnp.float32)
    for _ in range(3):
        piece = rest.astype(jnp.bfloat16)
        rest = rest - piece.astype(jnp.float32)
        back += lax.dot_general(
            chosen, piece, (((0,), (0,)), ((), ())), preferred_element_type=jnp.float32
        )
    total_ref[...] = back[:, :width]
    first = lax.broadcasted_iota(jnp.int32, (LANES, LANES), 0)
    second = lax.broadcasted_iota(jnp.int32, (LANES, LANES), 1)
    for start in range(0, back.shape[0], LANES):
        dens = back[start : start + LANES, width:]
        dens_ref[:, start : start + LANES] = jnp.sum(
            jnp.where(first == second, dens, 0.0), axis=0, keepdims=True
        )


def on_device(n_gr, n_gc, embeddings, cluster_ids):
    count, width = embeddings.shape
    size = count // n_gr
    own = lax.axis_index("gr").astype(jnp.int32).reshape(1)
    ids = cluster_ids.reshape(1, count)

    parts = pl.pallas_call(
        sort_kernel,
        out_shape=[jax.ShapeDtypeStruct((size, width), jnp.bfloat16)] * n_gr,
        in_specs=[SMEM, VMEM, VMEM],
        out_specs=[VMEM] * n_gr,
        compiler_params=GRANT,
        name="sort_rows",
    )(own, ids, embeddings)

    def along_gr(part, bits):
        return lax.ppermute(part, "gr", [(i, i ^ bits) for i in range(n_gr)])

    def along_gc(block, bits):
        return lax.ppermute(block, "gc", [(i, i ^ bits) for i in range(n_gc)])

    def cost(pairs):
        return pl.CostEstimate(
            flops=4 * pairs * width,
            bytes_accessed=0,
            transcendentals=pairs,
        )

    held = [parts[0]] + [along_gr(parts[k], k) for k in range(1, n_gr)]
    chunks = []
    for piece in held:
        near = [piece] + [along_gc(piece, bits) for bits in range(2, n_gc, 2)]
        same = jnp.concatenate(near, axis=0)
        chunks.append((same, along_gc(same, 1)))
    rows = jnp.concatenate(held, axis=0)
    early = [cols for chunk in chunks[:-1] for cols in chunk]

    total, dens = pl.pallas_call(
        first_kernel,
        out_shape=[
            jax.ShapeDtypeStruct((count, width), jnp.float32),
            jax.ShapeDtypeStruct((count, LANES), jnp.float32),
        ],
        in_specs=[VMEM] * (1 + len(early)),
        out_specs=[VMEM] * 2,
        compiler_params=GRANT,
        cost_estimate=cost(count * size * n_gc * (n_gr - 1)),
        name="early_sums",
    )(rows, *early)
    sums = pl.pallas_call(
        functools.partial(last_kernel, n_gr),
        out_shape=[jax.ShapeDtypeStruct((size, width + LANES), jnp.float32)] * n_gr,
        in_specs=[VMEM] * 5,
        out_specs=[VMEM] * n_gr,
        compiler_params=GRANT,
        cost_estimate=cost(count * size * n_gc),
        name="last_sums",
    )(rows, total, dens, *chunks[-1])

    back = [sums[0]] + [along_gr(sums[k], k) for k in range(1, n_gr)]
    neighbour_sum, density = pl.pallas_call(
        restore_kernel,
        out_shape=[
            jax.ShapeDtypeStruct((count, width), jnp.float32),
            jax.ShapeDtypeStruct((1, count), jnp.float32),
        ],
        in_specs=[SMEM, VMEM] + [VMEM] * n_gr,
        out_specs=[VMEM, VMEM],
        compiler_params=GRANT,
        name="restore_rows",
    )(own, ids, *back)
    return (neighbour_sum, density.reshape(count))


def solution(mesh):
    in_specs = (P(("gr", "gc"), None), P(("gr", "gc")))
    out_specs = (P(("gr", "gc"), None), P(("gr", "gc")))
    return jax.shard_map(
        functools.partial(on_device, mesh.shape["gr"], mesh.shape["gc"]),
        mesh=mesh,
        in_specs=in_specs,
        out_specs=out_specs,
        check_vma=False,
    )
```

profile of v0, /device:TPU:8, one launch (start us, length us, event | category | flops | bytes accessed | tf_op | source)
XLA Modules:
  0.0 64.1 jit_solution(7232388847491077785)
XLA Ops:
  0.6 0.7 %copy-done.1 = s32[256]{0:T(256)S(1)} copy-done((s32[256]{0:T(256)S(1)}, s32[256]{0:T(256)}, u32[]{:S(2)}) %copy-start.1) | copy-done | bytes 1048
  1.3 1.0 %copy-done = bf16[256,768]{1,0:T(8,128)(2,1)S(1)} copy-done((bf16[256,768]{1,0:T(8,128)(2,1)S(1)}, bf16[256,768]{1,0:T(8,128)(2,1)}, u32[]{:S(2)}) %copy-start) | copy-done | bytes 393240
  2.3 0.4 sort_rows.1
  2.7 1.6 %collective-permute-start.3 = (bf16[64,768]{1,0:T(8,128)(2,1)S(1)}, bf16[64,768]{1,0:T(8,128)(2,1)S(1)}, u32[]{:S(2)}, u32[]{:S(2)}) collective-permute-start(bf16[64,768]{1,0:T(8,128)(2,1)S(1)} %get-tuple-element.14), channel_id=1, source_target_pairs={{0,2},{1,3},{2,0},{3,1},{4,6},{5,7},{6,4},{7,5},{8,10},{9,11},{10,... | collective-permute-start | bytes 294920 | tf_op jit(solution)/shard_map/ppermute | solution.py:127
  4.3 1.5 %collective-permute-start.4 = (bf16[64,768]{1,0:T(8,128)(2,1)S(1)}, bf16[64,768]{1,0:T(8,128)(2,1)S(1)}, u32[]{:S(2)}, u32[]{:S(2)}) collective-permute-start(bf16[64,768]{1,0:T(8,128)(2,1)S(1)} %get-tuple-element.14), channel_id=1, source_target_pairs={{0,4},{1,5},{2,6},{3,7},{4,0},{5,1},{6,2},{7,3},{8,12},{9,13},{10,... | collective-permute-start | bytes 294920 | tf_op jit(solution)/shard_map/ppermute | solution.py:127
  5.8 0.5 collective-permute-start.5
  6.3 3.0 %collective-permute-start.1 = (bf16[64,768]{1,0:T(8,128)(2,1)S(1)}, bf16[64,768]{1,0:T(8,128)(2,1)S(1)}, u32[]{:S(2)}, u32[]{:S(2)}) collective-permute-start(bf16[64,768]{1,0:T(8,128)(2,1)S(1)} %get-tuple-element.16), channel_id=1, source_target_pairs={{0,16},{8,24},{16,0},{24,8},{1,17},{9,25},{17,1},{25,9},{2,18},{10... | collective-permute-start | bytes 294920 | tf_op jit(solution)/shard_map/ppermute | solution.py:124
  9.4 0.5 collective-permute-start.2
  10.0 1.4 %collective-permute-done.5 = bf16[64,768]{1,0:T(8,128)(2,1)S(1)} collective-permute-done((bf16[64,768]{1,0:T(8,128)(2,1)S(1)}, bf16[64,768]{1,0:T(8,128)(2,1)S(1)}, u32[]{:S(2)}, u32[]{:S(2)}) %collective-permute-start.5) | collective-permute-done | bytes 98336 | tf_op jit(solution)/shard_map/ppermute | solution.py:127
  11.4 4.1 %collective-permute-done.1 = bf16[64,768]{1,0:T(8,128)(2,1)S(1)} collective-permute-done((bf16[64,768]{1,0:T(8,128)(2,1)S(1)}, bf16[64,768]{1,0:T(8,128)(2,1)S(1)}, u32[]{:S(2)}, u32[]{:S(2)}) %collective-permute-start.1) | collective-permute-done | bytes 98336 | tf_op jit(solution)/shard_map/ppermute | solution.py:124
  15.5 1.5 %collective-permute-start.11 = (bf16[64,768]{1,0:T(8,128)(2,1)S(1)}, bf16[64,768]{1,0:T(8,128)(2,1)S(1)}, u32[]{:S(2)}, u32[]{:S(2)}) collective-permute-start(bf16[64,768]{1,0:T(8,128)(2,1)S(1)} %collective-permute-done.1), channel_id=1, source_target_pairs={{0,2},{1,3},{2,0},{3,1},{4,6},{5,7},{6,4},{7,5},{8,10},{9,11},{10,... | collective-permute-start | bytes 294920 | tf_op jit(solution)/shard_map/ppermute | solution.py:127
  17.0 1.5 %collective-permute-start.12 = (bf16[64,768]{1,0:T(8,128)(2,1)S(1)}, bf16[64,768]{1,0:T(8,128)(2,1)S(1)}, u32[]{:S(2)}, u32[]{:S(2)}) collective-permute-start(bf16[64,768]{1,0:T(8,128)(2,1)S(1)} %collective-permute-done.1), channel_id=1, source_target_pairs={{0,4},{1,5},{2,6},{3,7},{4,0},{5,1},{6,2},{7,3},{8,12},{9,13},{10,... | collective-permute-start | bytes 294920 | tf_op jit(solution)/shard_map/ppermute | solution.py:127
  18.5 0.5 collective-permute-start.13
  19.1 1.6 %collective-permute-start.7 = (bf16[64,768]{1,0:T(8,128)(2,1)S(1)}, bf16[64,768]{1,0:T(8,128)(2,1)S(1)}, u32[]{:S(2)}, u32[]{:S(2)}) collective-permute-start(bf16[64,768]{1,0:T(8,128)(2,1)S(1)} %collective-permute-done), channel_id=1, source_target_pairs={{0,2},{1,3},{2,0},{3,1},{4,6},{5,7},{6,4},{7,5},{8,10},{9,11},{10,... | collective-permute-start | bytes 294920 | tf_op jit(solution)/shard_map/ppermute | solution.py:127
  20.6 0.1 collective-permute-done.11
  20.7 1.5 %collective-permute-start.8 = (bf16[64,768]{1,0:T(8,128)(2,1)S(1)}, bf16[64,768]{1,0:T(8,128)(2,1)S(1)}, u32[]{:S(2)}, u32[]{:S(2)}) collective-permute-start(bf16[64,768]{1,0:T(8,128)(2,1)S(1)} %collective-permute-done), channel_id=1, source_target_pairs={{0,4},{1,5},{2,6},{3,7},{4,0},{5,1},{6,2},{7,3},{8,12},{9,13},{10,... | collective-permute-start | bytes 294920 | tf_op jit(solution)/shard_map/ppermute | solution.py:127
  22.2 1.3 %collective-permute-done.12 = bf16[64,768]{1,0:T(8,128)(2,1)S(1)} collective-permute-done((bf16[64,768]{1,0:T(8,128)(2,1)S(1)}, bf16[64,768]{1,0:T(8,128)(2,1)S(1)}, u32[]{:S(2)}, u32[]{:S(2)}) %collective-permute-start.12) | collective-permute-done | bytes 98336 | tf_op jit(solution)/shard_map/ppermute | solution.py:127
  23.5 2.1 %collective-permute-start.9 = (bf16[64,768]{1,0:T(8,128)(2,1)S(1)}, bf16[64,768]{1,0:T(8,128)(2,1)S(1)}, u32[]{:S(2)}, u32[]{:S(2)}) collective-permute-start(bf16[64,768]{1,0:T(8,128)(2,1)S(1)} %collective-permute-done), channel_id=1, source_target_pairs={{0,6},{1,7},{2,4},{3,5},{4,2},{5,3},{6,0},{7,1},{8,14},{9,15},{10,... | collective-permute-start | bytes 294920 | tf_op jit(solution)/shard_map/ppermute | solution.py:127
  25.6 2.1 %collective-permute-start.15 = (bf16[64,768]{1,0:T(8,128)(2,1)S(1)}, bf16[64,768]{1,0:T(8,128)(2,1)S(1)}, u32[]{:S(2)}, u32[]{:S(2)}) collective-permute-start(bf16[64,768]{1,0:T(8,128)(2,1)S(1)} %collective-permute-done.2), channel_id=1, source_target_pairs={{0,2},{1,3},{2,0},{3,1},{4,6},{5,7},{6,4},{7,5},{8,10},{9,11},{10,... | collective-permute-start | bytes 294920 | tf_op jit(solution)/shard_map/ppermute | solution.py:127
  27.8 1.5 %collective-permute-start.17 = (bf16[64,768]{1,0:T(8,128)(2,1)S(1)}, bf16[64,768]{1,0:T(8,128)(2,1)S(1)}, u32[]{:S(2)}, u32[]{:S(2)}) collective-permute-start(bf16[64,768]{1,0:T(8,128)(2,1)S(1)} %collective-permute-done.2), channel_id=1, source_target_pairs={{0,6},{1,7},{2,4},{3,5},{4,2},{5,3},{6,0},{7,1},{8,14},{9,15},{10,... | collective-permute-start | bytes 294920 | tf_op jit(solution)/shard_map/ppermute | solution.py:127
  29.4 1.8 %collective-permute-done.15 = bf16[64,768]{1,0:T(8,128)(2,1)S(1)} collective-permute-done((bf16[64,768]{1,0:T(8,128)(2,1)S(1)}, bf16[64,768]{1,0:T(8,128)(2,1)S(1)}, u32[]{:S(2)}, u32[]{:S(2)}) %collective-permute-start.15) | collective-permute-done | bytes 98336 | tf_op jit(solution)/shard_map/ppermute | solution.py:127
  31.3 1.1 %collective-permute-done.16 = bf16[64,768]{1,0:T(8,128)(2,1)S(1)} collective-permute-done((bf16[64,768]{1,0:T(8,128)(2,1)S(1)}, bf16[64,768]{1,0:T(8,128)(2,1)S(1)}, u32[]{:S(2)}, u32[]{:S(2)}) %collective-permute-start.16) | collective-permute-done | bytes 98336 | tf_op jit(solution)/shard_map/ppermute | solution.py:127
  32.4 1.0 %collective-permute-done.17 = bf16[64,768]{1,0:T(8,128)(2,1)S(1)} collective-permute-done((bf16[64,768]{1,0:T(8,128)(2,1)S(1)}, bf16[64,768]{1,0:T(8,128)(2,1)S(1)}, u32[]{:S(2)}, u32[]{:S(2)}) %collective-permute-start.17) | collective-permute-done | bytes 98336 | tf_op jit(solution)/shard_map/ppermute | solution.py:127
  33.6 2.3 %early_sums.1 = (f32[256,768]{1,0:T(8,128)S(1)}, f32[256,128]{1,0:T(8,128)S(1)}) custom-call(bf16[256,768]{1,0:T(8,128)(2,1)S(1)} %get-tuple-element.27.rows_ref, bf16[256,768]{1,0:T(8,128)(2,1)S(1)} %constant_dynamic-update-slice_fusion.4.refs_0_, bf16[256,768]{1,0:T(8,128)(2,1)S(1)} %collective-permute-done.6.refs_1_, ...), custom_call_target="tpu_custom_call" | custom-call | flops 1207959552 | tf_op jit(solution)/shard_map/early_sums/pallas_call | solution.py:145
  35.9 1.0 %last_sums.1 = (f32[64,896]{1,0:T(8,128)S(1)}, f32[64,896]{1,0:T(8,128)S(1)}, f32[64,896]{1,0:T(8,128)S(1)}, f32[64,896]{1,0:T(8,128)S(1)}) custom-call(bf16[256,768]{1,0:T(8,128)(2,1)S(1)} %get-tuple-element.27.rows_ref, f32[256,768]{1,0:T(8,128)S(1)} %get-tuple-element.18.total_ref, f32[256,128]{1,0:T(8,128)S(1)} %get-tuple-element.19.dens_ref, ...), custom_call_target="tpu_custom_call" | custom-call | flops 402653184 | tf_op jit(solution)/shard_map/last_sums/pallas_call | solution.py:157
  36.9 3.1 %collective-permute-start.19 = (f32[64,896]{1,0:T(8,128)S(1)}, f32[64,896]{1,0:T(8,128)S(1)}, u32[]{:S(2)}, u32[]{:S(2)}) collective-permute-start(f32[64,896]{1,0:T(8,128)S(1)} %get-tuple-element.21), channel_id=1, source_target_pairs={{0,8},{8,0},{16,24},{24,16},{1,9},{9,1},{17,25},{25,17},{2,10},{10... | collective-permute-start | bytes 688136 | tf_op jit(solution)/shard_map/ppermute | solution.py:124
  40.0 1.2 %collective-permute-start.20 = (f32[64,896]{1,0:T(8,128)S(1)}, f32[64,896]{1,0:T(8,128)S(1)}, u32[]{:S(2)}, u32[]{:S(2)}) collective-permute-start(f32[64,896]{1,0:T(8,128)S(1)} %get-tuple-element.22), channel_id=1, source_target_pairs={{0,16},{8,24},{16,0},{24,8},{1,17},{9,25},{17,1},{25,9},{2,18},{10... | collective-permute-start | bytes 688136 | tf_op jit(solution)/shard_map/ppermute | solution.py:124
  41.2 0.5 collective-permute-start.21
  41.7 8.4 %collective-permute-done.19.refs_1_ = f32[64,896]{1,0:T(8,128)S(1)} collective-permute-done((f32[64,896]{1,0:T(8,128)S(1)}, f32[64,896]{1,0:T(8,128)S(1)}, u32[]{:S(2)}, u32[]{:S(2)}) %collective-permute-start.19) | collective-permute-done | bytes 229408 | tf_op jit(solution)/shard_map/ppermute | solution.py:124
  50.1 6.9 %collective-permute-done.20.refs_2_ = f32[64,896]{1,0:T(8,128)S(1)} collective-permute-done((f32[64,896]{1,0:T(8,128)S(1)}, f32[64,896]{1,0:T(8,128)S(1)}, u32[]{:S(2)}, u32[]{:S(2)}) %collective-permute-start.20) | collective-permute-done | bytes 229408 | tf_op jit(solution)/shard_map/ppermute | solution.py:124
  57.0 5.4 %collective-permute-done.21.refs_3_ = f32[64,896]{1,0:T(8,128)S(1)} collective-permute-done((f32[64,896]{1,0:T(8,128)S(1)}, f32[64,896]{1,0:T(8,128)S(1)}, u32[]{:S(2)}, u32[]{:S(2)}) %collective-permute-start.21) | collective-permute-done | bytes 229408 | tf_op jit(solution)/shard_map/ppermute | solution.py:124
  62.4 1.7 %restore_rows.1 = (f32[256,768]{1,0:T(8,128)}, f32[1,256]{1,0:T(1,128)}) custom-call(s32[1]{0:T(128)} %bitcast.own_ref, s32[1,256]{1,0:T(1,128)S(1)} %bitcast.4, f32[64,896]{1,0:T(8,128)S(1)} %get-tuple-element.20.refs_0_, f32[64,896]{1,0:T(8,128)S(1)} %collective-permute-done.19.refs_1_, f32[64,896]{1,0:T(8,128)S(1)} %collective-permute-done.20.refs_2_, ...), custom_call_target="tpu_custom_call" | custom-call | tf_op jit(solution)/shard_map/restore_rows/pallas_call | solution.py:168
  (37 shorter events, 0.6 us)
Async XLA Ops:
  0.6 0.7 %copy-start.1 = (s32[256]{0:T(256)S(1)}, s32[256]{0:T(256)}, u32[]{:S(2)}) copy-start(s32[256]{0:T(256)} %param.3) | copy-start | bytes 3076
  1.3 1.0 %copy-start = (bf16[256,768]{1,0:T(8,128)(2,1)S(1)}, bf16[256,768]{1,0:T(8,128)(2,1)}, u32[]{:S(2)}) copy-start(bf16[256,768]{1,0:T(8,128)(2,1)} %rows_ref.1) | copy-start | bytes 1179652
  2.7 6.6 %collective-permute-start.3 = (bf16[64,768]{1,0:T(8,128)(2,1)S(1)}, bf16[64,768]{1,0:T(8,128)(2,1)S(1)}, u32[]{:S(2)}, u32[]{:S(2)}) collective-permute-start(bf16[64,768]{1,0:T(8,128)(2,1)S(1)} %get-tuple-element.14), channel_id=1, source_target_pairs={{0,2},{1,3},{2,0},{3,1},{4,6},{5,7},{6,4},{7,5},{8,10},{9,11},{10,... | collective-permute-start | bytes 294920 | tf_op jit(solution)/shard_map/ppermute | solution.py:127
  4.3 5.7 %collective-permute-start.4 = (bf16[64,768]{1,0:T(8,128)(2,1)S(1)}, bf16[64,768]{1,0:T(8,128)(2,1)S(1)}, u32[]{:S(2)}, u32[]{:S(2)}) collective-permute-start(bf16[64,768]{1,0:T(8,128)(2,1)S(1)} %get-tuple-element.14), channel_id=1, source_target_pairs={{0,4},{1,5},{2,6},{3,7},{4,0},{5,1},{6,2},{7,3},{8,12},{9,13},{10,... | collective-permute-start | bytes 294920 | tf_op jit(solution)/shard_map/ppermute | solution.py:127
  5.8 5.5 %collective-permute-start.5 = (bf16[64,768]{1,0:T(8,128)(2,1)S(1)}, bf16[64,768]{1,0:T(8,128)(2,1)S(1)}, u32[]{:S(2)}, u32[]{:S(2)}) collective-permute-start(bf16[64,768]{1,0:T(8,128)(2,1)S(1)} %get-tuple-element.14), channel_id=1, source_target_pairs={{0,6},{1,7},{2,4},{3,5},{4,2},{5,3},{6,0},{7,1},{8,14},{9,15},{10,... | collective-permute-start | bytes 294920 | tf_op jit(solution)/shard_map/ppermute | solution.py:127
  6.3 12.3 %collective-permute-start = (bf16[64,768]{1,0:T(8,128)(2,1)S(1)}, bf16[64,768]{1,0:T(8,128)(2,1)S(1)}, u32[]{:S(2)}, u32[]{:S(2)}) collective-permute-start(bf16[64,768]{1,0:T(8,128)(2,1)S(1)} %get-tuple-element.15), channel_id=1, source_target_pairs={{0,8},{8,0},{16,24},{24,16},{1,9},{9,1},{17,25},{25,17},{2,10},{10... | collective-permute-start | bytes 294920 | tf_op jit(solution)/shard_map/ppermute | solution.py:124
  6.3 9.2 %collective-permute-start.1 = (bf16[64,768]{1,0:T(8,128)(2,1)S(1)}, bf16[64,768]{1,0:T(8,128)(2,1)S(1)}, u32[]{:S(2)}, u32[]{:S(2)}) collective-permute-start(bf16[64,768]{1,0:T(8,128)(2,1)S(1)} %get-tuple-element.16), channel_id=1, source_target_pairs={{0,16},{8,24},{16,0},{24,8},{1,17},{9,25},{17,1},{25,9},{2,18},{10... | collective-permute-start | bytes 294920 | tf_op jit(solution)/shard_map/ppermute | solution.py:124
  9.4 9.7 %collective-permute-start.2 = (bf16[64,768]{1,0:T(8,128)(2,1)S(1)}, bf16[64,768]{1,0:T(8,128)(2,1)S(1)}, u32[]{:S(2)}, u32[]{:S(2)}) collective-permute-start(bf16[64,768]{1,0:T(8,128)(2,1)S(1)} %get-tuple-element.17), channel_id=1, source_target_pairs={{0,24},{8,16},{16,8},{24,0},{1,25},{9,17},{17,9},{25,1},{2,26},{10... | collective-permute-start | bytes 294920 | tf_op jit(solution)/shard_map/ppermute | solution.py:124
  11.3 22.2 %collective-permute-start.6 = (bf16[256,768]{1,0:T(8,128)(2,1)S(1)}, bf16[256,768]{1,0:T(8,128)(2,1)S(1)}, u32[]{:S(2)}, u32[]{:S(2)}) collective-permute-start(bf16[256,768]{1,0:T(8,128)(2,1)S(1)} %constant_dynamic-update-slice_fusion.4.refs_0_), channel_id=1, source_target_pairs={{0,1},{1,0},{2,3},{3,2},{4,5},{5,4},{6,7},{7,6},{8,9},{9,8},{10,11... | collective-permute-start | bytes 1179656 | tf_op jit(solution)/shard_map/ppermute | solution.py:127
  15.5 5.2 %collective-permute-start.11 = (bf16[64,768]{1,0:T(8,128)(2,1)S(1)}, bf16[64,768]{1,0:T(8,128)(2,1)S(1)}, u32[]{:S(2)}, u32[]{:S(2)}) collective-permute-start(bf16[64,768]{1,0:T(8,128)(2,1)S(1)} %collective-permute-done.1), channel_id=1, source_target_pairs={{0,2},{1,3},{2,0},{3,1},{4,6},{5,7},{6,4},{7,5},{8,10},{9,11},{10,... | collective-permute-start | bytes 294920 | tf_op jit(solution)/shard_map/ppermute | solution.py:127
  17.0 6.5 %collective-permute-start.12 = (bf16[64,768]{1,0:T(8,128)(2,1)S(1)}, bf16[64,768]{1,0:T(8,128)(2,1)S(1)}, u32[]{:S(2)}, u32[]{:S(2)}) collective-permute-start(bf16[64,768]{1,0:T(8,128)(2,1)S(1)} %collective-permute-done.1), channel_id=1, source_target_pairs={{0,4},{1,5},{2,6},{3,7},{4,0},{5,1},{6,2},{7,3},{8,12},{9,13},{10,... | collective-permute-start | bytes 294920 | tf_op jit(solution)/shard_map/ppermute | solution.py:127
  18.5 7.1 %collective-permute-start.13 = (bf16[64,768]{1,0:T(8,128)(2,1)S(1)}, bf16[64,768]{1,0:T(8,128)(2,1)S(1)}, u32[]{:S(2)}, u32[]{:S(2)}) collective-permute-start(bf16[64,768]{1,0:T(8,128)(2,1)S(1)} %collective-permute-done.1), channel_id=1, source_target_pairs={{0,6},{1,7},{2,4},{3,5},{4,2},{5,3},{6,0},{7,1},{8,14},{9,15},{10,... | collective-permute-start | bytes 294920 | tf_op jit(solution)/shard_map/ppermute | solution.py:127
  19.1 8.6 %collective-permute-start.7 = (bf16[64,768]{1,0:T(8,128)(2,1)S(1)}, bf16[64,768]{1,0:T(8,128)(2,1)S(1)}, u32[]{:S(2)}, u32[]{:S(2)}) collective-permute-start(bf16[64,768]{1,0:T(8,128)(2,1)S(1)} %collective-permute-done), channel_id=1, source_target_pairs={{0,2},{1,3},{2,0},{3,1},{4,6},{5,7},{6,4},{7,5},{8,10},{9,11},{10,... | collective-permute-start | bytes 294920 | tf_op jit(solution)/shard_map/ppermute | solution.py:127
  20.7 7.1 %collective-permute-start.8 = (bf16[64,768]{1,0:T(8,128)(2,1)S(1)}, bf16[64,768]{1,0:T(8,128)(2,1)S(1)}, u32[]{:S(2)}, u32[]{:S(2)}) collective-permute-start(bf16[64,768]{1,0:T(8,128)(2,1)S(1)} %collective-permute-done), channel_id=1, source_target_pairs={{0,4},{1,5},{2,6},{3,7},{4,0},{5,1},{6,2},{7,3},{8,12},{9,13},{10,... | collective-permute-start | bytes 294920 | tf_op jit(solution)/shard_map/ppermute | solution.py:127
  23.5 5.8 %collective-permute-start.9 = (bf16[64,768]{1,0:T(8,128)(2,1)S(1)}, bf16[64,768]{1,0:T(8,128)(2,1)S(1)}, u32[]{:S(2)}, u32[]{:S(2)}) collective-permute-start(bf16[64,768]{1,0:T(8,128)(2,1)S(1)} %collective-permute-done), channel_id=1, source_target_pairs={{0,6},{1,7},{2,4},{3,5},{4,2},{5,3},{6,0},{7,1},{8,14},{9,15},{10,... | collective-permute-start | bytes 294920 | tf_op jit(solution)/shard_map/ppermute | solution.py:127
  25.6 5.6 %collective-permute-start.15 = (bf16[64,768]{1,0:T(8,128)(2,1)S(1)}, bf16[64,768]{1,0:T(8,128)(2,1)S(1)}, u32[]{:S(2)}, u32[]{:S(2)}) collective-permute-start(bf16[64,768]{1,0:T(8,128)(2,1)S(1)} %collective-permute-done.2), channel_id=1, source_target_pairs={{0,2},{1,3},{2,0},{3,1},{4,6},{5,7},{6,4},{7,5},{8,10},{9,11},{10,... | collective-permute-start | bytes 294920 | tf_op jit(solution)/shard_map/ppermute | solution.py:127
  27.7 4.7 %collective-permute-start.16 = (bf16[64,768]{1,0:T(8,128)(2,1)S(1)}, bf16[64,768]{1,0:T(8,128)(2,1)S(1)}, u32[]{:S(2)}, u32[]{:S(2)}) collective-permute-start(bf16[64,768]{1,0:T(8,128)(2,1)S(1)} %collective-permute-done.2), channel_id=1, source_target_pairs={{0,4},{1,5},{2,6},{3,7},{4,0},{5,1},{6,2},{7,3},{8,12},{9,13},{10,... | collective-permute-start | bytes 294920 | tf_op jit(solution)/shard_map/ppermute | solution.py:127
  27.8 5.6 %collective-permute-start.17 = (bf16[64,768]{1,0:T(8,128)(2,1)S(1)}, bf16[64,768]{1,0:T(8,128)(2,1)S(1)}, u32[]{:S(2)}, u32[]{:S(2)}) collective-permute-start(bf16[64,768]{1,0:T(8,128)(2,1)S(1)} %collective-permute-done.2), channel_id=1, source_target_pairs={{0,6},{1,7},{2,4},{3,5},{4,2},{5,3},{6,0},{7,1},{8,14},{9,15},{10,... | collective-permute-start | bytes 294920 | tf_op jit(solution)/shard_map/ppermute | solution.py:127
  29.3 4.2 %collective-permute-start.14 = (bf16[256,768]{1,0:T(8,128)(2,1)S(1)}, bf16[256,768]{1,0:T(8,128)(2,1)S(1)}, u32[]{:S(2)}, u32[]{:S(2)}) collective-permute-start(bf16[256,768]{1,0:T(8,128)(2,1)S(1)} %constant_dynamic-update-slice_fusion.12.refs_4_), channel_id=1, source_target_pairs={{0,1},{1,0},{2,3},{3,2},{4,5},{5,4},{6,7},{7,6},{8,9},{9,8},{10,11... | collective-permute-start | bytes 1179656 | tf_op jit(solution)/shard_map/ppermute | solution.py:127
  31.2 2.3 %collective-permute-start.10 = (bf16[256,768]{1,0:T(8,128)(2,1)S(1)}, bf16[256,768]{1,0:T(8,128)(2,1)S(1)}, u32[]{:S(2)}, u32[]{:S(2)}) collective-permute-start(bf16[256,768]{1,0:T(8,128)(2,1)S(1)} %constant_dynamic-update-slice_fusion.8.refs_2_), channel_id=1, source_target_pairs={{0,1},{1,0},{2,3},{3,2},{4,5},{5,4},{6,7},{7,6},{8,9},{9,8},{10,11... | collective-permute-start | bytes 1179656 | tf_op jit(solution)/shard_map/ppermute | solution.py:127
  33.4 2.4 %collective-permute-start.18 = (bf16[256,768]{1,0:T(8,128)(2,1)S(1)}, bf16[256,768]{1,0:T(8,128)(2,1)S(1)}, u32[]{:S(2)}, u32[]{:S(2)}) collective-permute-start(bf16[256,768]{1,0:T(8,128)(2,1)S(1)} %constant_dynamic-update-slice_fusion.16.refs_0_), channel_id=1, source_target_pairs={{0,1},{1,0},{2,3},{3,2},{4,5},{5,4},{6,7},{7,6},{8,9},{9,8},{10,11... | collective-permute-start | bytes 1179656 | tf_op jit(solution)/shard_map/ppermute | solution.py:127
  36.9 13.2 %collective-permute-start.19 = (f32[64,896]{1,0:T(8,128)S(1)}, f32[64,896]{1,0:T(8,128)S(1)}, u32[]{:S(2)}, u32[]{:S(2)}) collective-permute-start(f32[64,896]{1,0:T(8,128)S(1)} %get-tuple-element.21), channel_id=1, source_target_pairs={{0,8},{8,0},{16,24},{24,16},{1,9},{9,1},{17,25},{25,17},{2,10},{10... | collective-permute-start | bytes 688136 | tf_op jit(solution)/shard_map/ppermute | solution.py:124
  40.0 17.0 %collective-permute-start.20 = (f32[64,896]{1,0:T(8,128)S(1)}, f32[64,896]{1,0:T(8,128)S(1)}, u32[]{:S(2)}, u32[]{:S(2)}) collective-permute-start(f32[64,896]{1,0:T(8,128)S(1)} %get-tuple-element.22), channel_id=1, source_target_pairs={{0,16},{8,24},{16,0},{24,8},{1,17},{9,25},{17,1},{25,9},{2,18},{10... | collective-permute-start | bytes 688136 | tf_op jit(solution)/shard_map/ppermute | solution.py:124
  41.2 21.2 %collective-permute-start.21 = (f32[64,896]{1,0:T(8,128)S(1)}, f32[64,896]{1,0:T(8,128)S(1)}, u32[]{:S(2)}, u32[]{:S(2)}) collective-permute-start(f32[64,896]{1,0:T(8,128)S(1)} %get-tuple-element.23), channel_id=1, source_target_pairs={{0,24},{8,16},{16,8},{24,0},{1,25},{9,17},{17,9},{25,1},{2,26},{10... | collective-permute-start | bytes 688136 | tf_op jit(solution)/shard_map/ppermute | solution.py:124
where the time goes:
time: 64.3 us; the launch traced here: 64.1 us
  waiting for transfers between devices  31.6 us (49%)
  starting transfers between devices  24.4 us (38%)
  Pallas kernels  5.37 us (8%)
  local copies, waits for them, and re-layouts  1.84 us (3%)
  between operations  0.83 us (1%)
    ppermute x6, waiting for transfers between devices, along_gr(): return lax.ppermute(part, 'gr', [(i, i ^ bits) for i in range(n_gr)])  24.8 us
    ppermute x16, starting transfers between devices, along_gc(): return lax.ppermute(block, 'gc', [(i, i ^ bits) for i in range(n_gc)])  16.1 us
    ppermute x6, starting transfers between devices, along_gr(): return lax.ppermute(part, 'gr', [(i, i ^ bits) for i in range(n_gr)])  8.36 us
    ppermute x16, waiting for transfers between devices, along_gc(): return lax.ppermute(block, 'gc', [(i, i ^ bits) for i in range(n_gc)])  6.77 us
    pallas_call x1, Pallas kernels, on_device(): pl.pallas_call(first_kernel, out_shape=[jax.ShapeDtypeStruct((count, widt...  2.31 us
    unnamed x17, local copies, waits for them, and re-layouts  1.8 us
    pallas_call x1, Pallas kernels, on_device(): pl.pallas_call(restore_kernel, out_shape=[jax.ShapeDtypeStruct((count, wi...  1.67 us
  transfers between devices with their start and end apart: 22, of which 11 were waited for; matrix products, arithmetic and copies ran while one was open for 0% of the time, Pallas kernels for 4%

commit v1 on v0

--- a/solution.py
+++ b/solution.py
@@ -44,8 +44,13 @@
 def add_columns(rows, col_refs, total, dens):
     count = rows.shape[0]
     scale = inverse_norms(rows) * (beta_scale * math.log2(math.e))
-    for col_ref in col_refs:
-        cols = col_ref[...]
+    blocks = [
+        (col_ref, start)
+        for col_ref in col_refs
+        for start in range(0, col_ref.shape[0], count)
+    ]
+    for col_ref, start in blocks:
+        cols = col_ref[start : start + count, :]
         size = cols.shape[0]
         first = lax.broadcasted_iota(jnp.int32, (size, size), 0)
         second = lax.broadcasted_iota(jnp.int32, (size, size), 1)
@@ -56,8 +61,8 @@
             rows, cols, (((1,), (1,)), ((), ())), preferred_element_type=jnp.float32
         )
         weight = jnp.exp2(raw * scale * col_inv - beta_scale * math.log2(math.e))
-        for start in range(0, size, LANES):
-            dens += weight[:, start : start + LANES]
+        for lane in range(0, size, LANES):
+            dens += weight[:, lane : lane + LANES]
         coef = (weight * col_inv).astype(jnp.bfloat16)
         total += jnp.dot(coef, cols, preferred_element_type=jnp.float32)
     return total, dens
@@ -123,8 +128,14 @@
     def along_gr(part, bits):
         return lax.ppermute(part, "gr", [(i, i ^ bits) for i in range(n_gr)])
 
-    def along_gc(block, bits):
-        return lax.ppermute(block, "gc", [(i, i ^ bits) for i in range(n_gc)])
+    bits = [1 << k for k in range(1, n_gc.bit_length() - 1)]
+
+    def in_plane(block, step):
+        pairs = [(i, i ^ bits[(step + i % 2) % len(bits)]) for i in range(n_gc)]
+        return lax.ppermute(block, "gc", pairs)
+
+    def other_core(block):
+        return lax.ppermute(block, "gc", [(i, i ^ 1) for i in range(n_gc)])
 
     def cost(pairs):
         return pl.CostEstimate(
@@ -134,13 +145,16 @@
         )
 
     held = [parts[0]] + [along_gr(parts[k], k) for k in range(1, n_gr)]
-    chunks = []
-    for piece in held:
-        near = [piece] + [along_gc(piece, bits) for bits in range(2, n_gc, 2)]
-        same = jnp.concatenate(near, axis=0)
-        chunks.append((same, along_gc(same, 1)))
+    half = n_gr // 2
+    first = jnp.concatenate(held[:half], axis=0)
+    for step in range(len(bits)):
+        first = jnp.concatenate([first, in_plane(first, step)], axis=0)
+    second = jnp.concatenate(held[half:], axis=0)
+    for step in range(len(bits) - 1):
+        second = jnp.concatenate([second, in_plane(second, step)], axis=0)
+    third = in_plane(second, len(bits) - 1)
     rows = jnp.concatenate(held, axis=0)
-    early = [cols for chunk in chunks[:-1] for cols in chunk]
+    early = [first, other_core(first), second, other_core(second)]
 
     total, dens = pl.pallas_call(
         first_kernel,
@@ -151,18 +165,20 @@
         in_specs=[VMEM] * (1 + len(early)),
         out_specs=[VMEM] * 2,
         compiler_params=GRANT,
-        cost_estimate=cost(count * size * n_gc * (n_gr - 1)),
+        cost_estimate=cost(count * sum(cols.shape[0] for cols in early)),
         name="early_sums",
     )(rows, *early)
+    third, total = lax.optimization_barrier((third, total))
+    late = [third, other_core(third)]
     sums = pl.pallas_call(
         functools.partial(last_kernel, n_gr),
         out_shape=[jax.ShapeDtypeStruct((size, width + LANES), jnp.float32)] * n_gr,
-        in_specs=[VMEM] * 5,
+        in_specs=[VMEM] * (3 + len(late)),
         out_specs=[VMEM] * n_gr,
         compiler_params=GRANT,
-        cost_estimate=cost(count * size * n_gc),
+        cost_estimate=cost(count * sum(cols.shape[0] for cols in late)),
         name="last_sums",
-    )(rows, total, dens, *chunks[-1])
+    )(rows, total, dens, *late)
 
     back = [sums[0]] + [along_gr(sums[k], k) for k in range(1, n_gr)]
     neighbour_sum, density = pl.pallas_call(

time: 64.3 us -> 65.9 us (1.025)
  the two profiles are of different devices: /device:TPU:8 before, /device:TPU:20 now
where the time goes in v1:
time: 65.9 us; the launch traced here: 65.7 us
  waiting for transfers between devices  46 us (70%)
  starting transfers between devices  11.7 us (18%)
  Pallas kernels  5.39 us (8%)
  local copies, waits for them, and re-layouts  1.78 us (3%)
  between operations  0.74 us (1%)
    ppermute x6, waiting for transfers between devices, along_gr(): return lax.ppermute(part, 'gr', [(i, i ^ bits) for i in range(n_gr)])  25.9 us
    ppermute x4, waiting for transfers between devices, in_plane(): return lax.ppermute(block, 'gc', pairs)  17.2 us
    ppermute x6, starting transfers between devices, along_gr(): return lax.ppermute(part, 'gr', [(i, i ^ bits) for i in range(n_gr)])  8.23 us
    ppermute x4, starting transfers between devices, in_plane(): return lax.ppermute(block, 'gc', pairs)  3.3 us
    ppermute x3, waiting for transfers between devices, other_core(): return lax.ppermute(block, 'gc', [(i, i ^ 1) for i in range(n_gc)])  2.86 us
    pallas_call x1, Pallas kernels, on_device(): pl.pallas_call(first_kernel, out_shape=[jax.ShapeDtypeStruct((count, widt...  2.32 us
    unnamed x9, local copies, waits for them, and re-layouts  1.74 us
    pallas_call x1, Pallas kernels, on_device(): pl.pallas_call(restore_kernel, out_shape=[jax.ShapeDtypeStruct((count, wi...  1.68 us
  transfers between devices with their start and end apart: 13, of which 11 were waited for; matrix products, arithmetic and copies ran while one was open for 0% of the time, Pallas kernels for 4%

profile of v1, /device:TPU:20, one launch (start us, length us, event | category | flops | bytes accessed | tf_op | source)
XLA Modules:
  0.0 65.7 jit_solution(3882302465434514208)
XLA Ops:
  0.6 0.7 %copy-done.1 = s32[256]{0:T(256)S(1)} copy-done((s32[256]{0:T(256)S(1)}, s32[256]{0:T(256)}, u32[]{:S(2)}) %copy-start.1) | copy-done | bytes 1048
  1.3 1.0 %copy-done = bf16[256,768]{1,0:T(8,128)(2,1)S(1)} copy-done((bf16[256,768]{1,0:T(8,128)(2,1)S(1)}, bf16[256,768]{1,0:T(8,128)(2,1)}, u32[]{:S(2)}) %copy-start) | copy-done | bytes 393240
  2.3 0.4 sort_rows.1
  2.7 1.6 %collective-permute-start = (bf16[64,768]{1,0:T(8,128)(2,1)S(1)}, bf16[64,768]{1,0:T(8,128)(2,1)S(1)}, u32[]{:S(2)}, u32[]{:S(2)}) collective-permute-start(bf16[64,768]{1,0:T(8,128)(2,1)S(1)} %get-tuple-element.17), channel_id=1, source_target_pairs={{0,8},{8,0},{16,24},{24,16},{1,9},{9,1},{17,25},{25,17},{2,10},{10... | collective-permute-start | bytes 294920 | tf_op jit(solution)/shard_map/ppermute | solution.py:129
  4.4 3.0 %collective-permute-done = bf16[64,768]{1,0:T(8,128)(2,1)S(1)} collective-permute-done((bf16[64,768]{1,0:T(8,128)(2,1)S(1)}, bf16[64,768]{1,0:T(8,128)(2,1)S(1)}, u32[]{:S(2)}, u32[]{:S(2)}) %collective-permute-start) | collective-permute-done | bytes 98336 | tf_op jit(solution)/shard_map/ppermute | solution.py:129
  7.4 1.6 %collective-permute-start.5 = (bf16[128,768]{1,0:T(8,128)(2,1)S(1)}, bf16[128,768]{1,0:T(8,128)(2,1)S(1)}, u32[]{:S(2)}, u32[]{:S(2)}) collective-permute-start(bf16[128,768]{1,0:T(8,128)(2,1)S(1)} %pad_maximum_fusion.2), channel_id=1, source_target_pairs={{0,2},{1,5},{2,0},{3,7},{4,6},{5,1},{6,4},{7,3},{8,10},{9,13},{10,... | collective-permute-start | bytes 589832 | tf_op jit(solution)/shard_map/ppermute | solution.py:135
  9.0 4.2 %collective-permute-done.5 = bf16[128,768]{1,0:T(8,128)(2,1)S(1)} collective-permute-done((bf16[128,768]{1,0:T(8,128)(2,1)S(1)}, bf16[128,768]{1,0:T(8,128)(2,1)S(1)}, u32[]{:S(2)}, u32[]{:S(2)}) %collective-permute-start.5) | collective-permute-done | bytes 196640 | tf_op jit(solution)/shard_map/ppermute | solution.py:135
  13.2 0.6 collective-permute-start.6
  13.8 0.1 collective-permute-start.1
  13.8 2.9 %collective-permute-start.2 = (bf16[64,768]{1,0:T(8,128)(2,1)S(1)}, bf16[64,768]{1,0:T(8,128)(2,1)S(1)}, u32[]{:S(2)}, u32[]{:S(2)}) collective-permute-start(bf16[64,768]{1,0:T(8,128)(2,1)S(1)} %get-tuple-element.19), channel_id=1, source_target_pairs={{0,24},{8,16},{16,8},{24,0},{1,25},{9,17},{17,9},{25,1},{2,26},{10... | collective-permute-start | bytes 294920 | tf_op jit(solution)/shard_map/ppermute | solution.py:129
  16.9 4.2 %collective-permute-done.6 = bf16[256,768]{1,0:T(8,128)(2,1)S(1)} collective-permute-done((bf16[256,768]{1,0:T(8,128)(2,1)S(1)}, bf16[256,768]{1,0:T(8,128)(2,1)S(1)}, u32[]{:S(2)}, u32[]{:S(2)}) %collective-permute-start.6) | collective-permute-done | bytes 393248 | tf_op jit(solution)/shard_map/ppermute | solution.py:135
  21.1 0.1 collective-permute-start.7
  21.1 0.0 collective-permute-done.1
  21.1 2.8 %collective-permute-done.2 = bf16[64,768]{1,0:T(8,128)(2,1)S(1)} collective-permute-done((bf16[64,768]{1,0:T(8,128)(2,1)S(1)}, bf16[64,768]{1,0:T(8,128)(2,1)S(1)}, u32[]{:S(2)}, u32[]{:S(2)}) %collective-permute-start.2) | collective-permute-done | bytes 98336 | tf_op jit(solution)/shard_map/ppermute | solution.py:129
  23.9 0.6 collective-permute-start.3
  24.6 5.1 %collective-permute-done.3 = bf16[128,768]{1,0:T(8,128)(2,1)S(1)} collective-permute-done((bf16[128,768]{1,0:T(8,128)(2,1)S(1)}, bf16[128,768]{1,0:T(8,128)(2,1)S(1)}, u32[]{:S(2)}, u32[]{:S(2)}) %collective-permute-start.3) | collective-permute-done | bytes 196640 | tf_op jit(solution)/shard_map/ppermute | solution.py:135
  29.7 0.1 collective-permute-start.8
  29.8 0.6 collective-permute-start.4
  30.3 1.1 %collective-permute-done.8.refs_3_ = bf16[256,768]{1,0:T(8,128)(2,1)S(1)} collective-permute-done((bf16[256,768]{1,0:T(8,128)(2,1)S(1)}, bf16[256,768]{1,0:T(8,128)(2,1)S(1)}, u32[]{:S(2)}, u32[]{:S(2)}) %collective-permute-start.8) | collective-permute-done | bytes 393248 | tf_op jit(solution)/shard_map/ppermute | solution.py:138
  31.5 0.0 collective-permute-done.7.refs_1_
  31.5 2.3 %early_sums.1 = (f32[256,768]{1,0:T(8,128)S(1)}, f32[256,128]{1,0:T(8,128)S(1)}) custom-call(bf16[256,768]{1,0:T(8,128)(2,1)S(1)} %get-tuple-element.35.rows_ref, bf16[512,768]{1,0:T(8,128)(2,1)S(1)} %constant_dynamic-update-slice_fusion.7.refs_0_, bf16[512,768]{1,0:T(8,128)(2,1)S(1)} %collective-permute-done.7.refs_1_, ...), custom_call_target="tpu_custom_call" | custom-call | flops 1207959552 | tf_op jit(solution)/shard_map/early_sums/pallas_call | solution.py:159
  33.8 3.8 %collective-permute-done.4.refs_0_ = bf16[256,768]{1,0:T(8,128)(2,1)S(1)} collective-permute-done((bf16[256,768]{1,0:T(8,128)(2,1)S(1)}, bf16[256,768]{1,0:T(8,128)(2,1)S(1)}, u32[]{:S(2)}, u32[]{:S(2)}) %collective-permute-start.4) | collective-permute-done | bytes 393248 | tf_op jit(solution)/shard_map/ppermute | solution.py:135
  37.6 0.0 collective-permute-start.9
  37.6 1.7 %collective-permute-done.9.refs_1_ = bf16[256,768]{1,0:T(8,128)(2,1)S(1)} collective-permute-done((bf16[256,768]{1,0:T(8,128)(2,1)S(1)}, bf16[256,768]{1,0:T(8,128)(2,1)S(1)}, u32[]{:S(2)}, u32[]{:S(2)}) %collective-permute-start.9) | collective-permute-done | bytes 393248 | tf_op jit(solution)/shard_map/ppermute | solution.py:138
  39.3 1.0 %last_sums.1 = (f32[64,896]{1,0:T(8,128)S(1)}, f32[64,896]{1,0:T(8,128)S(1)}, f32[64,896]{1,0:T(8,128)S(1)}, f32[64,896]{1,0:T(8,128)S(1)}) custom-call(bf16[256,768]{1,0:T(8,128)(2,1)S(1)} %get-tuple-element.35.rows_ref, f32[256,768]{1,0:T(8,128)S(1)} %get-tuple-element.21.total_ref, f32[256,128]{1,0:T(8,128)S(1)} %get-tuple-element.22.dens_ref, ...), custom_call_target="tpu_custom_call" | custom-call | flops 402653184 | tf_op jit(solution)/shard_map/last_sums/pallas_call | solution.py:173
  40.3 0.2 collective-permute-start.10
  40.5 1.1 %collective-permute-start.11 = (f32[64,896]{1,0:T(8,128)S(1)}, f32[64,896]{1,0:T(8,128)S(1)}, u32[]{:S(2)}, u32[]{:S(2)}) collective-permute-start(f32[64,896]{1,0:T(8,128)S(1)} %get-tuple-element.26), channel_id=1, source_target_pairs={{0,16},{8,24},{16,0},{24,8},{1,17},{9,25},{17,1},{25,9},{2,18},{10... | collective-permute-start | bytes 688136 | tf_op jit(solution)/shard_map/ppermute | solution.py:129
  41.6 2.3 %collective-permute-start.12 = (f32[64,896]{1,0:T(8,128)S(1)}, f32[64,896]{1,0:T(8,128)S(1)}, u32[]{:S(2)}, u32[]{:S(2)}) collective-permute-start(f32[64,896]{1,0:T(8,128)S(1)} %get-tuple-element.27), channel_id=1, source_target_pairs={{0,24},{8,16},{16,8},{24,0},{1,25},{9,17},{17,9},{25,1},{2,26},{10... | collective-permute-start | bytes 688136 | tf_op jit(solution)/shard_map/ppermute | solution.py:129
  43.9 5.0 %collective-permute-done.10.refs_1_ = f32[64,896]{1,0:T(8,128)S(1)} collective-permute-done((f32[64,896]{1,0:T(8,128)S(1)}, f32[64,896]{1,0:T(8,128)S(1)}, u32[]{:S(2)}, u32[]{:S(2)}) %collective-permute-start.10) | collective-permute-done | bytes 229408 | tf_op jit(solution)/shard_map/ppermute | solution.py:129
  48.8 8.5 %collective-permute-done.11.refs_2_ = f32[64,896]{1,0:T(8,128)S(1)} collective-permute-done((f32[64,896]{1,0:T(8,128)S(1)}, f32[64,896]{1,0:T(8,128)S(1)}, u32[]{:S(2)}, u32[]{:S(2)}) %collective-permute-start.11) | collective-permute-done | bytes 229408 | tf_op jit(solution)/shard_map/ppermute | solution.py:129
  57.3 6.7 %collective-permute-done.12.refs_3_ = f32[64,896]{1,0:T(8,128)S(1)} collective-permute-done((f32[64,896]{1,0:T(8,128)S(1)}, f32[64,896]{1,0:T(8,128)S(1)}, u32[]{:S(2)}, u32[]{:S(2)}) %collective-permute-start.12) | collective-permute-done | bytes 229408 | tf_op jit(solution)/shard_map/ppermute | solution.py:129
  64.0 1.7 %restore_rows.1 = (f32[256,768]{1,0:T(8,128)}, f32[1,256]{1,0:T(1,128)}) custom-call(s32[1]{0:T(128)} %bitcast.own_ref, s32[1,256]{1,0:T(1,128)S(1)} %bitcast.4, f32[64,896]{1,0:T(8,128)S(1)} %get-tuple-element.24.refs_0_, f32[64,896]{1,0:T(8,128)S(1)} %collective-permute-done.10.refs_1_, f32[64,896]{1,0:T(8,128)S(1)} %collective-permute-done.11.refs_2_, ...), custom_call_target="tpu_custom_call" | custom-call | tf_op jit(solution)/shard_map/restore_rows/pallas_call | solution.py:184
  (12 shorter events, 0.2 us)
Async XLA Ops:
  0.6 0.7 %copy-start.1 = (s32[256]{0:T(256)S(1)}, s32[256]{0:T(256)}, u32[]{:S(2)}) copy-start(s32[256]{0:T(256)} %param.3) | copy-start | bytes 3076
  1.3 1.0 %copy-start = (bf16[256,768]{1,0:T(8,128)(2,1)S(1)}, bf16[256,768]{1,0:T(8,128)(2,1)}, u32[]{:S(2)}) copy-start(bf16[256,768]{1,0:T(8,128)(2,1)} %rows_ref.1) | copy-start | bytes 1179652
  2.7 4.7 %collective-permute-start = (bf16[64,768]{1,0:T(8,128)(2,1)S(1)}, bf16[64,768]{1,0:T(8,128)(2,1)S(1)}, u32[]{:S(2)}, u32[]{:S(2)}) collective-permute-start(bf16[64,768]{1,0:T(8,128)(2,1)S(1)} %get-tuple-element.17), channel_id=1, source_target_pairs={{0,8},{8,0},{16,24},{24,16},{1,9},{9,1},{17,25},{25,17},{2,10},{10... | collective-permute-start | bytes 294920 | tf_op jit(solution)/shard_map/ppermute | solution.py:129
  7.4 5.7 %collective-permute-start.5 = (bf16[128,768]{1,0:T(8,128)(2,1)S(1)}, bf16[128,768]{1,0:T(8,128)(2,1)S(1)}, u32[]{:S(2)}, u32[]{:S(2)}) collective-permute-start(bf16[128,768]{1,0:T(8,128)(2,1)S(1)} %pad_maximum_fusion.2), channel_id=1, source_target_pairs={{0,2},{1,5},{2,0},{3,7},{4,6},{5,1},{6,4},{7,3},{8,10},{9,13},{10,... | collective-permute-start | bytes 589832 | tf_op jit(solution)/shard_map/ppermute | solution.py:135
  13.2 7.8 %collective-permute-start.6 = (bf16[256,768]{1,0:T(8,128)(2,1)S(1)}, bf16[256,768]{1,0:T(8,128)(2,1)S(1)}, u32[]{:S(2)}, u32[]{:S(2)}) collective-permute-start(bf16[256,768]{1,0:T(8,128)(2,1)S(1)} %pad_maximum_fusion), channel_id=1, source_target_pairs={{0,4},{1,3},{2,6},{3,1},{4,0},{5,7},{6,2},{7,5},{8,12},{9,11},{10,... | collective-permute-start | bytes 1179656 | tf_op jit(solution)/shard_map/ppermute | solution.py:135
  13.8 7.4 %collective-permute-start.1 = (bf16[64,768]{1,0:T(8,128)(2,1)S(1)}, bf16[64,768]{1,0:T(8,128)(2,1)S(1)}, u32[]{:S(2)}, u32[]{:S(2)}) collective-permute-start(bf16[64,768]{1,0:T(8,128)(2,1)S(1)} %get-tuple-element.18), channel_id=1, source_target_pairs={{0,16},{8,24},{16,0},{24,8},{1,17},{9,25},{17,1},{25,9},{2,18},{10... | collective-permute-start | bytes 294920 | tf_op jit(solution)/shard_map/ppermute | solution.py:129
  13.8 10.1 %collective-permute-start.2 = (bf16[64,768]{1,0:T(8,128)(2,1)S(1)}, bf16[64,768]{1,0:T(8,128)(2,1)S(1)}, u32[]{:S(2)}, u32[]{:S(2)}) collective-permute-start(bf16[64,768]{1,0:T(8,128)(2,1)S(1)} %get-tuple-element.19), channel_id=1, source_target_pairs={{0,24},{8,16},{16,8},{24,0},{1,25},{9,17},{17,9},{25,1},{2,26},{10... | collective-permute-start | bytes 294920 | tf_op jit(solution)/shard_map/ppermute | solution.py:129
  21.1 10.4 %collective-permute-start.7 = (bf16[512,768]{1,0:T(8,128)(2,1)S(1)}, bf16[512,768]{1,0:T(8,128)(2,1)S(1)}, u32[]{:S(2)}, u32[]{:S(2)}) collective-permute-start(bf16[512,768]{1,0:T(8,128)(2,1)S(1)} %constant_dynamic-update-slice_fusion.7.refs_0_), channel_id=1, source_target_pairs={{0,1},{1,0},{2,3},{3,2},{4,5},{5,4},{6,7},{7,6},{8,9},{9,8},{10,11... | collective-permute-start | bytes 2359304 | tf_op jit(solution)/shard_map/ppermute | solution.py:138
  23.9 5.7 %collective-permute-start.3 = (bf16[128,768]{1,0:T(8,128)(2,1)S(1)}, bf16[128,768]{1,0:T(8,128)(2,1)S(1)}, u32[]{:S(2)}, u32[]{:S(2)}) collective-permute-start(bf16[128,768]{1,0:T(8,128)(2,1)S(1)} %pad_maximum_fusion.1), channel_id=1, source_target_pairs={{0,2},{1,5},{2,0},{3,7},{4,6},{5,1},{6,4},{7,3},{8,10},{9,13},{10,... | collective-permute-start | bytes 589832 | tf_op jit(solution)/shard_map/ppermute | solution.py:135
  29.7 1.8 %collective-permute-start.8 = (bf16[256,768]{1,0:T(8,128)(2,1)S(1)}, bf16[256,768]{1,0:T(8,128)(2,1)S(1)}, u32[]{:S(2)}, u32[]{:S(2)}) collective-permute-start(bf16[256,768]{1,0:T(8,128)(2,1)S(1)} %constant_dynamic-update-slice_fusion.4.refs_2_), channel_id=1, source_target_pairs={{0,1},{1,0},{2,3},{3,2},{4,5},{5,4},{6,7},{7,6},{8,9},{9,8},{10,11... | collective-permute-start | bytes 1179656 | tf_op jit(solution)/shard_map/ppermute | solution.py:138
  29.8 7.8 %collective-permute-start.4 = (bf16[256,768]{1,0:T(8,128)(2,1)S(1)}, bf16[256,768]{1,0:T(8,128)(2,1)S(1)}, u32[]{:S(2)}, u32[]{:S(2)}) collective-permute-start(bf16[256,768]{1,0:T(8,128)(2,1)S(1)} %constant_dynamic-update-slice_fusion.4.refs_2_), channel_id=1, source_target_pairs={{0,4},{1,3},{2,6},{3,1},{4,0},{5,7},{6,2},{7,5},{8,12},{9,11},{10,... | collective-permute-start | bytes 1179656 | tf_op jit(solution)/shard_map/ppermute | solution.py:135
  37.6 1.7 %collective-permute-start.9 = (bf16[256,768]{1,0:T(8,128)(2,1)S(1)}, bf16[256,768]{1,0:T(8,128)(2,1)S(1)}, u32[]{:S(2)}, u32[]{:S(2)}) collective-permute-start(bf16[256,768]{1,0:T(8,128)(2,1)S(1)} %collective-permute-done.4.refs_0_), channel_id=1, source_target_pairs={{0,1},{1,0},{2,3},{3,2},{4,5},{5,4},{6,7},{7,6},{8,9},{9,8},{10,11... | collective-permute-start | bytes 1179656 | tf_op jit(solution)/shard_map/ppermute | solution.py:138
  40.3 8.5 %collective-permute-start.10 = (f32[64,896]{1,0:T(8,128)S(1)}, f32[64,896]{1,0:T(8,128)S(1)}, u32[]{:S(2)}, u32[]{:S(2)}) collective-permute-start(f32[64,896]{1,0:T(8,128)S(1)} %get-tuple-element.25), channel_id=1, source_target_pairs={{0,8},{8,0},{16,24},{24,16},{1,9},{9,1},{17,25},{25,17},{2,10},{10... | collective-permute-start | bytes 688136 | tf_op jit(solution)/shard_map/ppermute | solution.py:129
  40.5 16.8 %collective-permute-start.11 = (f32[64,896]{1,0:T(8,128)S(1)}, f32[64,896]{1,0:T(8,128)S(1)}, u32[]{:S(2)}, u32[]{:S(2)}) collective-permute-start(f32[64,896]{1,0:T(8,128)S(1)} %get-tuple-element.26), channel_id=1, source_target_pairs={{0,16},{8,24},{16,0},{24,8},{1,17},{9,25},{17,1},{25,9},{2,18},{10... | collective-permute-start | bytes 688136 | tf_op jit(solution)/shard_map/ppermute | solution.py:129
  41.6 22.4 %collective-permute-start.12 = (f32[64,896]{1,0:T(8,128)S(1)}, f32[64,896]{1,0:T(8,128)S(1)}, u32[]{:S(2)}, u32[]{:S(2)}) collective-permute-start(f32[64,896]{1,0:T(8,128)S(1)} %get-tuple-element.27), channel_id=1, source_target_pairs={{0,24},{8,16},{16,8},{24,0},{1,25},{9,17},{17,9},{25,1},{2,26},{10... | collective-permute-start | bytes 688136 | tf_op jit(solution)/shard_map/ppermute | solution.py:129

commit v2 on v0

v2 whole, which is shorter than its diff:
```python
import functools
import math

import jax
import jax.numpy as jnp
from jax import lax
from jax.experimental import pallas as pl
from jax.experimental.pallas import tpu as pltpu
from jax.sharding import PartitionSpec as P

beta_scale = 16.0
LANES = 128
EXTRA = 8
TOP = 14.0
VMEM = pl.BlockSpec(memory_space=pltpu.VMEM)
SMEM = pl.BlockSpec(memory_space=pltpu.SMEM)
GRANT = pltpu.CompilerParams(vmem_limit_bytes=40 * 1024 * 1024)


def diagonal(count):
    first = lax.broadcasted_iota(jnp.int32, (count, count), 0)
    second = lax.broadcasted_iota(jnp.int32, (count, count), 1)
    return first == second


def as_row(column):
    return jnp.sum(
        jnp.where(diagonal(column.shape[0]), column, jnp.zeros_like(column)),
        axis=0,
        keepdims=True,
    )


def as_column(row):
    return jnp.sum(
        jnp.where(diagonal(row.shape[1]), row, jnp.zeros_like(row)),
        axis=1,
        keepdims=True,
    )


def placement(own, ids, groups):
    count = ids.shape[1]
    first = lax.broadcasted_iota(jnp.int32, (count, count), 0)
    second = lax.broadcasted_iota(jnp.int32, (count, count), 1)
    earlier = jnp.where((as_column(ids) == ids) & (first < second), 1, 0)
    rank = jnp.sum(earlier, axis=0, keepdims=True)
    slot = (ids ^ own) * (count // groups) + rank
    return jnp.where(first == slot, 1.0, 0.0)


def sort_kernel(own_ref, ids_ref, rows_ref, *out_refs):
    groups = len(out_refs)
    chosen = placement(own_ref[0], ids_ref[...], groups).astype(jnp.bfloat16)
    ordered = jnp.dot(chosen, rows_ref[...], preferred_element_type=jnp.float32)
    ordered = ordered.astype(jnp.bfloat16)
    size = ordered.shape[0] // groups
    for k, out_ref in enumerate(out_refs):
        out_ref[...] = ordered[k * size : (k + 1) * size, :]


def inverse_norms(rows):
    wide = rows.astype(jnp.float32)
    return lax.rsqrt(jnp.sum(wide * wide, axis=1, keepdims=True) + 1e-06)


def add_columns(rows, col_refs, total, dens):
    count = rows.shape[0]
    scale = inverse_norms(rows) * (beta_scale * math.log2(math.e))
    blocks = [
        (col_ref, start)
        for col_ref in col_refs
        for start in range(0, col_ref.shape[0], count)
    ]
    for col_ref, start in blocks:
        cols = col_ref[start : start + count, :]
        col_inv = as_row(inverse_norms(cols))
        raw = lax.dot_general(
            rows, cols, (((1,), (1,)), ((), ())), preferred_element_type=jnp.float32
        )
        weight = jnp.exp2(raw * scale * col_inv - beta_scale * math.log2(math.e))
        for lane in range(0, count, LANES):
            dens += weight[:, lane : lane + LANES]
        coef = (weight * col_inv).astype(jnp.bfloat16)
        total += jnp.dot(coef, cols, preferred_element_type=jnp.float32)
    return total, dens


def first_kernel(rows_ref, *refs):
    col_refs, (total_ref, dens_ref) = refs[:-2], refs[-2:]
    total = jnp.zeros(total_ref.shape, jnp.float32)
    dens = jnp.zeros(dens_ref.shape, jnp.float32)
    total, dens = add_columns(rows_ref[...], col_refs, total, dens)
    total_ref[...] = total
    dens_ref[...] = dens


def exponent(value):
    return jnp.floor(jnp.log2(jnp.maximum(value, 1e-37)))


def last_kernel(own_ref, rows_ref, total_ref, dens_ref, *refs):
    col_refs, out_ref = refs[:-1], refs[-1]
    groups, padded, width = out_ref.shape
    size = padded - EXTRA
    total, dens = add_columns(rows_ref[...], col_refs, total_ref[...], dens_ref[...])
    dens = jnp.sum(dens, axis=1, keepdims=True)
    power = exponent(jnp.max(jnp.abs(total), axis=1, keepdims=True))
    total = total * jnp.exp2(TOP - power)
    dens_power = exponent(dens)
    part = dens * jnp.exp2(-dens_power)
    aside = [power, dens_power]
    for k in range(3):
        piece = part.astype(jnp.bfloat16).astype(jnp.float32)
        aside.append(piece * 2.0 ** (8 * k))
        part = part - piece
    for k in range(groups):
        slot = own_ref[0] ^ k
        rows = slice(k * size, (k + 1) * size)
        out_ref[slot, :size, :] = total[rows, :]
        out_ref[slot, size:, :] = jnp.zeros((EXTRA, width), jnp.float32)
        for line, column in enumerate(aside):
            out_ref[slot, size + line : size + line + 1, :size] = as_row(column[rows, :])


def restore_kernel(ids_ref, parts_ref, total_ref, dens_ref):
    groups, padded, width = parts_ref.shape
    size = padded - EXTRA
    chosen = placement(0, ids_ref[...], groups)
    sums, dens = [], []
    for k in range(groups):
        power, dens_power, *pieces = [
            as_column(parts_ref[k, size + line : size + line + 1, :size])
            for line in range(5)
        ]
        sums.append(parts_ref[k, :size, :] * jnp.exp2(power - TOP))
        part = sum(piece * 2.0 ** (-8 * j) for j, piece in enumerate(pieces))
        dens.append(part * jnp.exp2(dens_power))
    dens_ref[...] = jnp.sum(
        chosen * jnp.concatenate(dens, axis=0), axis=0, keepdims=True
    )
    rest = jnp.concatenate(sums, axis=0)
    chosen = chosen.astype(jnp.bfloat16)
    back = jnp.zeros(rest.shape, jnp.float32)
    for _ in range(2):
        piece = rest.astype(jnp.bfloat16)
        rest = rest - piece.astype(jnp.float32)
        back += lax.dot_general(
            chosen, piece, (((0,), (0,)), ((), ())), preferred_element_type=jnp.float32
        )
    total_ref[...] = back


def on_device(n_gr, n_gc, embeddings, cluster_ids):
    count, width = embeddings.shape
    size = count // n_gr
    own = lax.axis_index("gr").astype(jnp.int32).reshape(1)
    ids = cluster_ids.reshape(1, count)

    parts = pl.pallas_call(
        sort_kernel,
        out_shape=[jax.ShapeDtypeStruct((size, width), jnp.bfloat16)] * n_gr,
        in_specs=[SMEM, VMEM, VMEM],
        out_specs=[VMEM] * n_gr,
        compiler_params=GRANT,
        name="sort_rows",
    )(own, ids, embeddings)

    def along_gr(part, bits):
        return lax.ppermute(part, "gr", [(i, i ^ bits) for i in range(n_gr)])

    def along_gc(block, bits):
        return lax.ppermute(block, "gc", [(i, i ^ bits) for i in range(n_gc)])

    def cost(pairs):
        return pl.CostEstimate(
            flops=4 * pairs * width,
            bytes_accessed=0,
            transcendentals=pairs,
        )

    held = [parts[0]] + [along_gr(parts[k], k) for k in range(1, n_gr)]
    half = n_gr // 2
    chunks = []
    for pieces in (held[:half], held[half:]):
        block = jnp.concatenate(pieces, axis=0)
        near = [block] + [along_gc(block, bits) for bits in range(2, n_gc, 2)]
        same = jnp.concatenate(near, axis=0)
        chunks.append([same, along_gc(same, 1)])
    rows = jnp.concatenate(held, axis=0)

    total, dens = pl.pallas_call(
        first_kernel,
        out_shape=[
            jax.ShapeDtypeStruct((count, width), jnp.float32),
            jax.ShapeDtypeStruct((count, LANES), jnp.float32),
        ],
        in_specs=[VMEM] * 3,
        out_specs=[VMEM] * 2,
        compiler_params=GRANT,
        cost_estimate=cost(count * count * n_gc // 2),
        name="early_sums",
    )(rows, *chunks[0])
    sums = pl.pallas_call(
        last_kernel,
        out_shape=jax.ShapeDtypeStruct((n_gr, size + EXTRA, width), jnp.float32),
        in_specs=[SMEM] + [VMEM] * 5,
        out_specs=VMEM,
        compiler_params=GRANT,
        cost_estimate=cost(count * count * n_gc // 2),
        name="last_sums",
    )(own, rows, total, dens, *chunks[1])

    back = lax.all_to_all(sums.astype(jnp.float16), "gr", 0, 0)
    neighbour_sum, density = pl.pallas_call(
        restore_kernel,
        out_shape=[
            jax.ShapeDtypeStruct((count, width), jnp.float32),
            jax.ShapeDtypeStruct((1, count), jnp.float32),
        ],
        in_specs=[VMEM, VMEM],
        out_specs=[VMEM, VMEM],
        compiler_params=GRANT,
        name="restore_rows",
    )(ids, back.astype(jnp.float32))
    return (neighbour_sum, density.reshape(count))


def solution(mesh):
    in_specs = (P(("gr", "gc"), None), P(("gr", "gc")))
    out_specs = (P(("gr", "gc"), None), P(("gr", "gc")))
    return jax.shard_map(
        functools.partial(on_device, mesh.shape["gr"], mesh.shape["gc"]),
        mesh=mesh,
        in_specs=in_specs,
        out_specs=out_specs,
        check_vma=False,
    )
```

time: 64.3 us -> 53.7 us (0.84)
  the two profiles are of different devices: /device:TPU:8 before, /device:TPU:0 now
where the time goes in v2:
time: 53.7 us; the launch traced here: 53.5 us
  blocking collectives  16.5 us (31%)
  starting transfers between devices  15 us (28%)
  waiting for transfers between devices  14.2 us (26%)
  Pallas kernels  5.2 us (10%)
  local copies, waits for them, and re-layouts  1.83 us (3%)
  between operations  0.77 us (1%)
    all_to_all x1, blocking collectives, on_device(): back = lax.all_to_all(sums.astype(jnp.float16), 'gr', 0, 0)  16.5 us
    ppermute x8, waiting for transfers between devices, along_gc(): return lax.ppermute(block, 'gc', [(i, i ^ bits) for i in range(n_gc)])  10.7 us
    ppermute x8, starting transfers between devices, along_gc(): return lax.ppermute(block, 'gc', [(i, i ^ bits) for i in range(n_gc)])  9.29 us
    ppermute x3, starting transfers between devices, along_gr(): return lax.ppermute(part, 'gr', [(i, i ^ bits) for i in range(n_gr)])  5.68 us
    ppermute x3, waiting for transfers between devices, along_gr(): return lax.ppermute(part, 'gr', [(i, i ^ bits) for i in range(n_gr)])  3.53 us
    unnamed x10, local copies, waits for them, and re-layouts  1.76 us
    pallas_call x1, Pallas kernels, on_device(): pl.pallas_call(first_kernel, out_shape=[jax.ShapeDtypeStruct((count, widt...  1.72 us
    pallas_call x1, Pallas kernels, on_device(): pl.pallas_call(last_kernel, out_shape=jax.ShapeDtypeStruct((n_gr, size +...  1.58 us
  transfers between devices with their start and end apart: 11, of which 7 were waited for; matrix products, arithmetic and copies ran while one was open for 0% of the time, Pallas kernels for 3%

profile of v2, /device:TPU:0, one launch (start us, length us, event | category | flops | bytes accessed | tf_op | source)
XLA Modules:
  0.0 53.5 jit_solution(8943335598935910154)
XLA Ops:
  0.6 0.0 copy-start.1
  0.6 0.7 %copy-done.1 = s32[256]{0:T(256)S(1)} copy-done((s32[256]{0:T(256)S(1)}, s32[256]{0:T(256)}, u32[]{:S(2)}) %copy-start.1) | copy-done | bytes 1048
  1.3 0.0 copy-start
  1.3 1.0 %copy-done = bf16[256,768]{1,0:T(8,128)(2,1)S(1)} copy-done((bf16[256,768]{1,0:T(8,128)(2,1)S(1)}, bf16[256,768]{1,0:T(8,128)(2,1)}, u32[]{:S(2)}) %copy-start) | copy-done | bytes 393240
  2.3 0.4 sort_rows.1
  2.7 4.1 %collective-permute-start.1 = (bf16[64,768]{1,0:T(8,128)(2,1)S(1)}, bf16[64,768]{1,0:T(8,128)(2,1)S(1)}, u32[]{:S(2)}, u32[]{:S(2)}) collective-permute-start(bf16[64,768]{1,0:T(8,128)(2,1)S(1)} %get-tuple-element.12), channel_id=1, source_target_pairs={{0,16},{8,24},{16,0},{24,8},{1,17},{9,25},{17,1},{25,9},{2,18},{10... | collective-permute-start | bytes 294920 | tf_op jit(solution)/shard_map/ppermute | solution.py:170
  6.8 1.6 %collective-permute-start = (bf16[64,768]{1,0:T(8,128)(2,1)S(1)}, bf16[64,768]{1,0:T(8,128)(2,1)S(1)}, u32[]{:S(2)}, u32[]{:S(2)}) collective-permute-start(bf16[64,768]{1,0:T(8,128)(2,1)S(1)} %get-tuple-element.11), channel_id=1, source_target_pairs={{0,8},{8,0},{16,24},{24,16},{1,9},{9,1},{17,25},{25,17},{2,10},{10... | collective-permute-start | bytes 294920 | tf_op jit(solution)/shard_map/ppermute | solution.py:170
  8.4 0.0 collective-permute-start.2
  8.4 3.5 %collective-permute-done = bf16[64,768]{1,0:T(8,128)(2,1)S(1)} collective-permute-done((bf16[64,768]{1,0:T(8,128)(2,1)S(1)}, bf16[64,768]{1,0:T(8,128)(2,1)S(1)}, u32[]{:S(2)}, u32[]{:S(2)}) %collective-permute-start) | collective-permute-done | bytes 98336 | tf_op jit(solution)/shard_map/ppermute | solution.py:170
  12.0 1.6 %collective-permute-start.3 = (bf16[128,768]{1,0:T(8,128)(2,1)S(1)}, bf16[128,768]{1,0:T(8,128)(2,1)S(1)}, u32[]{:S(2)}, u32[]{:S(2)}) collective-permute-start(bf16[128,768]{1,0:T(8,128)(2,1)S(1)} %get-tuple-element.24), channel_id=1, source_target_pairs={{0,2},{1,3},{2,0},{3,1},{4,6},{5,7},{6,4},{7,5},{8,10},{9,11},{10,... | collective-permute-start | bytes 589832 | tf_op jit(solution)/shard_map/ppermute | solution.py:173
  13.5 1.5 %collective-permute-start.4 = (bf16[128,768]{1,0:T(8,128)(2,1)S(1)}, bf16[128,768]{1,0:T(8,128)(2,1)S(1)}, u32[]{:S(2)}, u32[]{:S(2)}) collective-permute-start(bf16[128,768]{1,0:T(8,128)(2,1)S(1)} %get-tuple-element.24), channel_id=1, source_target_pairs={{0,4},{1,5},{2,6},{3,7},{4,0},{5,1},{6,2},{7,3},{8,12},{9,13},{10,... | collective-permute-start | bytes 589832 | tf_op jit(solution)/shard_map/ppermute | solution.py:173
  15.0 0.5 collective-permute-start.5
  15.5 0.0 collective-permute-done.1
  15.6 0.0 collective-permute-done.2
  15.6 1.6 %collective-permute-start.7 = (bf16[128,768]{1,0:T(8,128)(2,1)S(1)}, bf16[128,768]{1,0:T(8,128)(2,1)S(1)}, u32[]{:S(2)}, u32[]{:S(2)}) collective-permute-start(bf16[128,768]{1,0:T(8,128)(2,1)S(1)} %get-tuple-element.18), channel_id=1, source_target_pairs={{0,2},{1,3},{2,0},{3,1},{4,6},{5,7},{6,4},{7,5},{8,10},{9,11},{10,... | collective-permute-start | bytes 589832 | tf_op jit(solution)/shard_map/ppermute | solution.py:173
  17.2 1.5 %collective-permute-start.8 = (bf16[128,768]{1,0:T(8,128)(2,1)S(1)}, bf16[128,768]{1,0:T(8,128)(2,1)S(1)}, u32[]{:S(2)}, u32[]{:S(2)}) collective-permute-start(bf16[128,768]{1,0:T(8,128)(2,1)S(1)} %get-tuple-element.18), channel_id=1, source_target_pairs={{0,4},{1,5},{2,6},{3,7},{4,0},{5,1},{6,2},{7,3},{8,12},{9,13},{10,... | collective-permute-start | bytes 589832 | tf_op jit(solution)/shard_map/ppermute | solution.py:173
  18.7 1.1 %collective-permute-done.3 = bf16[128,768]{1,0:T(8,128)(2,1)S(1)} collective-permute-done((bf16[128,768]{1,0:T(8,128)(2,1)S(1)}, bf16[128,768]{1,0:T(8,128)(2,1)S(1)}, u32[]{:S(2)}, u32[]{:S(2)}) %collective-permute-start.3) | collective-permute-done | bytes 196640 | tf_op jit(solution)/shard_map/ppermute | solution.py:173
  19.8 2.5 %collective-permute-start.9 = (bf16[128,768]{1,0:T(8,128)(2,1)S(1)}, bf16[128,768]{1,0:T(8,128)(2,1)S(1)}, u32[]{:S(2)}, u32[]{:S(2)}) collective-permute-start(bf16[128,768]{1,0:T(8,128)(2,1)S(1)} %get-tuple-element.18), channel_id=1, source_target_pairs={{0,6},{1,7},{2,4},{3,5},{4,2},{5,3},{6,0},{7,1},{8,14},{9,15},{10,... | collective-permute-start | bytes 589832 | tf_op jit(solution)/shard_map/ppermute | solution.py:173
  22.3 2.3 %collective-permute-done.4 = bf16[128,768]{1,0:T(8,128)(2,1)S(1)} collective-permute-done((bf16[128,768]{1,0:T(8,128)(2,1)S(1)}, bf16[128,768]{1,0:T(8,128)(2,1)S(1)}, u32[]{:S(2)}, u32[]{:S(2)}) %collective-permute-start.4) | collective-permute-done | bytes 196640 | tf_op jit(solution)/shard_map/ppermute | solution.py:173
  24.6 0.5 collective-permute-done.5
  25.1 0.1 collective-permute-start.6
  25.2 3.0 %collective-permute-done.7 = bf16[128,768]{1,0:T(8,128)(2,1)S(1)} collective-permute-done((bf16[128,768]{1,0:T(8,128)(2,1)S(1)}, bf16[128,768]{1,0:T(8,128)(2,1)S(1)}, u32[]{:S(2)}, u32[]{:S(2)}) %collective-permute-start.7) | collective-permute-done | bytes 196640 | tf_op jit(solution)/shard_map/ppermute | solution.py:173
  28.1 3.3 %collective-permute-done.8 = bf16[128,768]{1,0:T(8,128)(2,1)S(1)} collective-permute-done((bf16[128,768]{1,0:T(8,128)(2,1)S(1)}, bf16[128,768]{1,0:T(8,128)(2,1)S(1)}, u32[]{:S(2)}, u32[]{:S(2)}) %collective-permute-start.8) | collective-permute-done | bytes 196640 | tf_op jit(solution)/shard_map/ppermute | solution.py:173
  31.5 0.0 collective-permute-done.9
  31.5 0.1 collective-permute-start.10
  31.6 0.0 collective-permute-done.6.refs_1_
  31.6 1.7 %early_sums.1 = (f32[256,768]{1,0:T(8,128)S(1)}, f32[256,128]{1,0:T(8,128)S(1)}) custom-call(bf16[256,768]{1,0:T(8,128)(2,1)S(1)} %get-tuple-element.20.rows_ref, bf16[512,768]{1,0:T(8,128)(2,1)S(1)} %constant_dynamic-update-slice_fusion.6.refs_0_, bf16[512,768]{1,0:T(8,128)(2,1)S(1)} %collective-permute-done.6.refs_1_), custom_call_target="tpu_custom_call" | custom-call | flops 805306368 | tf_op jit(solution)/shard_map/early_sums/pallas_call | solution.py:192
  33.3 0.5 %collective-permute-done.10.refs_1_ = bf16[512,768]{1,0:T(8,128)(2,1)S(1)} collective-permute-done((bf16[512,768]{1,0:T(8,128)(2,1)S(1)}, bf16[512,768]{1,0:T(8,128)(2,1)S(1)}, u32[]{:S(2)}, u32[]{:S(2)}) %collective-permute-start.10) | collective-permute-done | bytes 786464 | tf_op jit(solution)/shard_map/ppermute | solution.py:173
  33.9 1.6 %last_sums.1 = f32[4,72,768]{2,1,0:T(8,128)S(1)} custom-call(s32[1]{0:T(128)} %bitcast.1.own_ref, bf16[256,768]{1,0:T(8,128)(2,1)S(1)} %get-tuple-element.20.rows_ref, f32[256,768]{1,0:T(8,128)S(1)} %get-tuple-element.14.total_ref, f32[256,128]{1,0:T(8,128)S(1)} %get-tuple-element.15.dens_ref, ...), custom_call_target="tpu_custom_call" | custom-call | flops 805306368 | tf_op jit(solution)/shard_map/last_sums/pallas_call | solution.py:204
  35.5 16.5 %all_to_all.5 = f16[4,72,768]{2,1,0:T(8,128)(2,1)S(1)} all-to-all(f16[4,72,768]{2,1,0:T(8,128)(2,1)S(1)} %convert_element_type.6), channel_id=1, replica_groups=mesh['gr'=4,'gc'=8] {'gr'}, dimensions={0} | all-to-all | bytes 884736 | tf_op jit(solution)/shard_map/all_to_all | solution.py:214
  52.0 0.1 convert_element_type.7.parts_ref
  52.0 1.5 %restore_rows.1 = (f32[256,768]{1,0:T(8,128)}, f32[1,256]{1,0:T(1,128)}) custom-call(s32[1,256]{1,0:T(1,128)S(1)} %bitcast.4, f32[4,72,768]{2,1,0:T(8,128)S(1)} %convert_element_type.7.parts_ref), custom_call_target="tpu_custom_call" | custom-call | tf_op jit(solution)/shard_map/restore_rows/pallas_call | solution.py:215
  (11 shorter events, 0.2 us)
Async XLA Ops:
  0.6 0.7 %copy-start.1 = (s32[256]{0:T(256)S(1)}, s32[256]{0:T(256)}, u32[]{:S(2)}) copy-start(s32[256]{0:T(256)} %param.3) | copy-start | bytes 3076
  1.3 1.0 %copy-start = (bf16[256,768]{1,0:T(8,128)(2,1)S(1)}, bf16[256,768]{1,0:T(8,128)(2,1)}, u32[]{:S(2)}) copy-start(bf16[256,768]{1,0:T(8,128)(2,1)} %rows_ref.1) | copy-start | bytes 1179652
  2.7 12.8 %collective-permute-start.1 = (bf16[64,768]{1,0:T(8,128)(2,1)S(1)}, bf16[64,768]{1,0:T(8,128)(2,1)S(1)}, u32[]{:S(2)}, u32[]{:S(2)}) collective-permute-start(bf16[64,768]{1,0:T(8,128)(2,1)S(1)} %get-tuple-element.12), channel_id=1, source_target_pairs={{0,16},{8,24},{16,0},{24,8},{1,17},{9,25},{17,1},{25,9},{2,18},{10... | collective-permute-start | bytes 294920 | tf_op jit(solution)/shard_map/ppermute | solution.py:170
  6.8 5.1 %collective-permute-start = (bf16[64,768]{1,0:T(8,128)(2,1)S(1)}, bf16[64,768]{1,0:T(8,128)(2,1)S(1)}, u32[]{:S(2)}, u32[]{:S(2)}) collective-permute-start(bf16[64,768]{1,0:T(8,128)(2,1)S(1)} %get-tuple-element.11), channel_id=1, source_target_pairs={{0,8},{8,0},{16,24},{24,16},{1,9},{9,1},{17,25},{25,17},{2,10},{10... | collective-permute-start | bytes 294920 | tf_op jit(solution)/shard_map/ppermute | solution.py:170
  8.4 7.2 %collective-permute-start.2 = (bf16[64,768]{1,0:T(8,128)(2,1)S(1)}, bf16[64,768]{1,0:T(8,128)(2,1)S(1)}, u32[]{:S(2)}, u32[]{:S(2)}) collective-permute-start(bf16[64,768]{1,0:T(8,128)(2,1)S(1)} %get-tuple-element.13), channel_id=1, source_target_pairs={{0,24},{8,16},{16,8},{24,0},{1,25},{9,17},{17,9},{25,1},{2,26},{10... | collective-permute-start | bytes 294920 | tf_op jit(solution)/shard_map/ppermute | solution.py:170
  12.0 7.8 %collective-permute-start.3 = (bf16[128,768]{1,0:T(8,128)(2,1)S(1)}, bf16[128,768]{1,0:T(8,128)(2,1)S(1)}, u32[]{:S(2)}, u32[]{:S(2)}) collective-permute-start(bf16[128,768]{1,0:T(8,128)(2,1)S(1)} %get-tuple-element.24), channel_id=1, source_target_pairs={{0,2},{1,3},{2,0},{3,1},{4,6},{5,7},{6,4},{7,5},{8,10},{9,11},{10,... | collective-permute-start | bytes 589832 | tf_op jit(solution)/shard_map/ppermute | solution.py:173
  13.5 11.1 %collective-permute-start.4 = (bf16[128,768]{1,0:T(8,128)(2,1)S(1)}, bf16[128,768]{1,0:T(8,128)(2,1)S(1)}, u32[]{:S(2)}, u32[]{:S(2)}) collective-permute-start(bf16[128,768]{1,0:T(8,128)(2,1)S(1)} %get-tuple-element.24), channel_id=1, source_target_pairs={{0,4},{1,5},{2,6},{3,7},{4,0},{5,1},{6,2},{7,3},{8,12},{9,13},{10,... | collective-permute-start | bytes 589832 | tf_op jit(solution)/shard_map/ppermute | solution.py:173
  15.0 10.0 %collective-permute-start.5 = (bf16[128,768]{1,0:T(8,128)(2,1)S(1)}, bf16[128,768]{1,0:T(8,128)(2,1)S(1)}, u32[]{:S(2)}, u32[]{:S(2)}) collective-permute-start(bf16[128,768]{1,0:T(8,128)(2,1)S(1)} %get-tuple-element.24), channel_id=1, source_target_pairs={{0,6},{1,7},{2,4},{3,5},{4,2},{5,3},{6,0},{7,1},{8,14},{9,15},{10,... | collective-permute-start | bytes 589832 | tf_op jit(solution)/shard_map/ppermute | solution.py:173
  15.6 12.5 %collective-permute-start.7 = (bf16[128,768]{1,0:T(8,128)(2,1)S(1)}, bf16[128,768]{1,0:T(8,128)(2,1)S(1)}, u32[]{:S(2)}, u32[]{:S(2)}) collective-permute-start(bf16[128,768]{1,0:T(8,128)(2,1)S(1)} %get-tuple-element.18), channel_id=1, source_target_pairs={{0,2},{1,3},{2,0},{3,1},{4,6},{5,7},{6,4},{7,5},{8,10},{9,11},{10,... | collective-permute-start | bytes 589832 | tf_op jit(solution)/shard_map/ppermute | solution.py:173
  17.2 14.3 %collective-permute-start.8 = (bf16[128,768]{1,0:T(8,128)(2,1)S(1)}, bf16[128,768]{1,0:T(8,128)(2,1)S(1)}, u32[]{:S(2)}, u32[]{:S(2)}) collective-permute-start(bf16[128,768]{1,0:T(8,128)(2,1)S(1)} %get-tuple-element.18), channel_id=1, source_target_pairs={{0,4},{1,5},{2,6},{3,7},{4,0},{5,1},{6,2},{7,3},{8,12},{9,13},{10,... | collective-permute-start | bytes 589832 | tf_op jit(solution)/shard_map/ppermute | solution.py:173
  19.8 11.7 %collective-permute-start.9 = (bf16[128,768]{1,0:T(8,128)(2,1)S(1)}, bf16[128,768]{1,0:T(8,128)(2,1)S(1)}, u32[]{:S(2)}, u32[]{:S(2)}) collective-permute-start(bf16[128,768]{1,0:T(8,128)(2,1)S(1)} %get-tuple-element.18), channel_id=1, source_target_pairs={{0,6},{1,7},{2,4},{3,5},{4,2},{5,3},{6,0},{7,1},{8,14},{9,15},{10,... | collective-permute-start | bytes 589832 | tf_op jit(solution)/shard_map/ppermute | solution.py:173
  25.1 6.5 %collective-permute-start.6 = (bf16[512,768]{1,0:T(8,128)(2,1)S(1)}, bf16[512,768]{1,0:T(8,128)(2,1)S(1)}, u32[]{:S(2)}, u32[]{:S(2)}) collective-permute-start(bf16[512,768]{1,0:T(8,128)(2,1)S(1)} %constant_dynamic-update-slice_fusion.6.refs_0_), channel_id=1, source_target_pairs={{0,1},{1,0},{2,3},{3,2},{4,5},{5,4},{6,7},{7,6},{8,9},{9,8},{10,11... | collective-permute-start | bytes 2359304 | tf_op jit(solution)/shard_map/ppermute | solution.py:173
  31.5 2.4 %collective-permute-start.10 = (bf16[512,768]{1,0:T(8,128)(2,1)S(1)}, bf16[512,768]{1,0:T(8,128)(2,1)S(1)}, u32[]{:S(2)}, u32[]{:S(2)}) collective-permute-start(bf16[512,768]{1,0:T(8,128)(2,1)S(1)} %constant_dynamic-update-slice_fusion.13.refs_0_), channel_id=1, source_target_pairs={{0,1},{1,0},{2,3},{3,2},{4,5},{5,4},{6,7},{7,6},{8,9},{9,8},{10,11... | collective-permute-start | bytes 2359304 | tf_op jit(solution)/shard_map/ppermute | solution.py:173

commit v3 on v2

--- a/solution.py
+++ b/solution.py
@@ -99,9 +99,9 @@
     return jnp.floor(jnp.log2(jnp.maximum(value, 1e-37)))
 
 
-def last_kernel(own_ref, rows_ref, total_ref, dens_ref, *refs):
-    col_refs, out_ref = refs[:-1], refs[-1]
-    groups, padded, width = out_ref.shape
+def last_kernel(groups, rows_ref, total_ref, dens_ref, *refs):
+    col_refs, out_refs = refs[:-groups], refs[-groups:]
+    padded, width = out_refs[0].shape
     size = padded - EXTRA
     total, dens = add_columns(rows_ref[...], col_refs, total_ref[...], dens_ref[...])
     dens = jnp.sum(dens, axis=1, keepdims=True)
@@ -114,26 +114,26 @@
         piece = part.astype(jnp.bfloat16).astype(jnp.float32)
         aside.append(piece * 2.0 ** (8 * k))
         part = part - piece
-    for k in range(groups):
-        slot = own_ref[0] ^ k
+    for k, out_ref in enumerate(out_refs):
         rows = slice(k * size, (k + 1) * size)
-        out_ref[slot, :size, :] = total[rows, :]
-        out_ref[slot, size:, :] = jnp.zeros((EXTRA, width), jnp.float32)
+        out_ref[:size, :] = total[rows, :]
+        out_ref[size:, :] = jnp.zeros((EXTRA, width), jnp.float32)
         for line, column in enumerate(aside):
-            out_ref[slot, size + line : size + line + 1, :size] = as_row(column[rows, :])
-
-
-def restore_kernel(ids_ref, parts_ref, total_ref, dens_ref):
-    groups, padded, width = parts_ref.shape
-    size = padded - EXTRA
-    chosen = placement(0, ids_ref[...], groups)
+            out_ref[size + line : size + line + 1, :size] = as_row(column[rows, :])
+
+
+def restore_kernel(own_ref, ids_ref, *refs):
+    part_refs, (total_ref, dens_ref) = refs[:-2], refs[-2:]
+    groups = len(part_refs)
+    size = part_refs[0].shape[0] - EXTRA
+    chosen = placement(own_ref[0], ids_ref[...], groups)
     sums, dens = [], []
-    for k in range(groups):
+    for part_ref in part_refs:
         power, dens_power, *pieces = [
-            as_column(parts_ref[k, size + line : size + line + 1, :size])
+            as_column(part_ref[size + line : size + line + 1, :size])
             for line in range(5)
         ]
-        sums.append(parts_ref[k, :size, :] * jnp.exp2(power - TOP))
+        sums.append(part_ref[:size, :] * jnp.exp2(power - TOP))
         part = sum(piece * 2.0 ** (-8 * j) for j, piece in enumerate(pieces))
         dens.append(part * jnp.exp2(dens_power))
     dens_ref[...] = jnp.sum(
@@ -169,25 +169,42 @@
     def along_gr(part, bits):
         return lax.ppermute(part, "gr", [(i, i ^ bits) for i in range(n_gr)])
 
-    def along_gc(block, bits):
-        return lax.ppermute(block, "gc", [(i, i ^ bits) for i in range(n_gc)])
-
-    def cost(pairs):
+    bits = [1 << k for k in range(1, n_gc.bit_length() - 1)]
+
+    def in_plane(block, step):
+        pairs = [(i, i ^ bits[(step + i % 2) % len(bits)]) for i in range(n_gc)]
+        return lax.ppermute(block, "gc", pairs)
+
+    def other_core(block):
+        return lax.ppermute(block, "gc", [(i, i ^ 1) for i in range(n_gc)])
+
+    def doubled(block, steps):
+        for step in range(steps):
+            block = jnp.concatenate([block, in_plane(block, step)], axis=0)
+        return block
+
+    def cost(*blocks):
+        pairs = count * sum(block.shape[0] for block in blocks)
         return pl.CostEstimate(
             flops=4 * pairs * width,
             bytes_accessed=0,
             transcendentals=pairs,
         )
 
-    held = [parts[0]] + [along_gr(parts[k], k) for k in range(1, n_gr)]
-    half = n_gr // 2
-    chunks = []
-    for pieces in (held[:half], held[half:]):
-        block = jnp.concatenate(pieces, axis=0)
-        near = [block] + [along_gc(block, bits) for bits in range(2, n_gc, 2)]
-        same = jnp.concatenate(near, axis=0)
-        chunks.append([same, along_gc(same, 1)])
+    held = [None] * n_gr
+    held[0] = parts[0]
+    for k in sorted(range(1, n_gr), reverse=True):
+        held[k] = along_gr(parts[k], k)
+    start = doubled(held[0], len(bits))
+    second = doubled(held[1], len(bits) - 1)
+    second, others = lax.optimization_barrier((second, held[2:]))
+    second = jnp.concatenate([second, in_plane(second, len(bits) - 1)], axis=0)
+    start = jnp.concatenate([start, second], axis=0)
+    rest = doubled(jnp.concatenate(others, axis=0), len(bits) - 1)
+    last = in_plane(rest, len(bits) - 1)
     rows = jnp.concatenate(held, axis=0)
+    near = jnp.concatenate([start, rest], axis=0)
+    early = [near, other_core(near)]
 
     total, dens = pl.pallas_call(
         first_kernel,
@@ -195,34 +212,41 @@
             jax.ShapeDtypeStruct((count, width), jnp.float32),
             jax.ShapeDtypeStruct((count, LANES), jnp.float32),
         ],
-        in_specs=[VMEM] * 3,
+        in_specs=[VMEM] * (1 + len(early)),
         out_specs=[VMEM] * 2,
         compiler_params=GRANT,
-        cost_estimate=cost(count * count * n_gc // 2),
+        cost_estimate=cost(*early),
         name="early_sums",
-    )(rows, *chunks[0])
+    )(rows, *early)
+    last, total = lax.optimization_barrier((last, total))
+    late = [last, other_core(last)]
     sums = pl.pallas_call(
-        last_kernel,
-        out_shape=jax.ShapeDtypeStruct((n_gr, size + EXTRA, width), jnp.float32),
-        in_specs=[SMEM] + [VMEM] * 5,
-        out_specs=VMEM,
-        compiler_params=GRANT,
-        cost_estimate=cost(count * count * n_gc // 2),
+        functools.partial(last_kernel, n_gr),
+        out_shape=[jax.ShapeDtypeStruct((size + EXTRA, width), jnp.float32)] * n_gr,
+        in_specs=[VMEM] * 5,
+        out_specs=[VMEM] * n_gr,
+        compiler_params=GRANT,
+        cost_estimate=cost(*late),
         name="last_sums",
-    )(own, rows, total, dens, *chunks[1])
-
-    back = lax.all_to_all(sums.astype(jnp.float16), "gr", 0, 0)
+    )(rows, total, dens, *late)
+
+    sent = [part.astype(jnp.float16) for part in sums]
+    back = [None] * n_gr
+    back[0] = sent[0]
+    for k in sorted(range(1, n_gr), reverse=True):
+        back[k] = along_gr(sent[k], k)
+    back = [part.astype(jnp.float32) for part in back]
     neighbour_sum, density = pl.pallas_call(
         restore_kernel,
         out_shape=[
             jax.ShapeDtypeStruct((count, width), jnp.float32),
             jax.ShapeDtypeStruct((1, count), jnp.float32),
         ],
-        in_specs=[VMEM, VMEM],
+        in_specs=[SMEM, VMEM] + [VMEM] * n_gr,
         out_specs=[VMEM, VMEM],
         compiler_params=GRANT,
         name="restore_rows",
-    )(ids, back.astype(jnp.float32))
+    )(own, ids, *back)
     return (neighbour_sum, density.reshape(count))
 
 

time: 53.7 us -> 50.9 us (0.948)
  blocking collectives: 16.5 us -> 0 us
  waiting for transfers between devices: 14.2 us -> 24.6 us
  starting transfers between devices: 15 us -> 18 us
    all_to_all x1 -> x0, blocking collectives: 16.5 us -> none  [on_device(): back = lax.all_to_all(sums.astype(jnp.float16), 'gr', 0, 0)]
    ppermute x3 -> x6, waiting for transfers between devices: 3.53 us -> 9.87 us  [along_gr(): return lax.ppermute(part, 'gr', [(i, i ^ bits) for i in range(n_gr)])]
    ppermute x8, waiting for transfers between devices: 10.7 us -> 14.8 us  [the longest x6 11.4 us: in_plane(): return lax.ppermute(block, 'gc', pairs)]
    ppermute x3 -> x6, starting transfers between devices: 5.68 us -> 9.6 us  [along_gr(): return lax.ppermute(part, 'gr', [(i, i ^ bits) for i in range(n_gr)])]
    ppermute x8, starting transfers between devices: 9.29 us -> 8.36 us  [the longest x6 8.28 us: in_plane(): return lax.ppermute(block, 'gc', pairs)]
    pallas_call x1, Pallas kernels: 1.72 us -> 2.31 us  [on_device(): pl.pallas_call(first_kernel, out_shape=[jax.ShapeDtypeStruct((count, widt...]
    unnamed x10 -> x15, local copies, waits for them, and re-layouts: 1.76 us -> 1.77 us
  transfers between devices with their start and end apart: 11 -> 14, of which waited for: 7 -> 8; matrix products, arithmetic and copies ran while one was open for 0% -> 0% of each run, Pallas kernels for 3% -> 5%
where the time goes in v3:
time: 50.9 us; the launch traced here: 50.7 us
  waiting for transfers between devices  24.6 us (48%)
  starting transfers between devices  18 us (35%)
  Pallas kernels  5.35 us (11%)
  local copies, waits for them, and re-layouts  1.79 us (4%)
  between operations  0.83 us (2%)
    ppermute x6, waiting for transfers between devices, in_plane(): return lax.ppermute(block, 'gc', pairs)  11.4 us
    ppermute x6, waiting for transfers between devices, along_gr(): return lax.ppermute(part, 'gr', [(i, i ^ bits) for i in range(n_gr)])  9.87 us
    ppermute x6, starting transfers between devices, along_gr(): return lax.ppermute(part, 'gr', [(i, i ^ bits) for i in range(n_gr)])  9.6 us
    ppermute x6, starting transfers between devices, in_plane(): return lax.ppermute(block, 'gc', pairs)  8.28 us
    ppermute x2, waiting for transfers between devices, other_core(): return lax.ppermute(block, 'gc', [(i, i ^ 1) for i in range(n_gc)])  3.39 us
    pallas_call x1, Pallas kernels, on_device(): pl.pallas_call(first_kernel, out_shape=[jax.ShapeDtypeStruct((count, widt...  2.31 us
    unnamed x15, local copies, waits for them, and re-layouts  1.77 us
    pallas_call x1, Pallas kernels, on_device(): pl.pallas_call(restore_kernel, out_shape=[jax.ShapeDtypeStruct((count, wi...  1.5 us
  transfers between devices with their start and end apart: 14, of which 8 were waited for; matrix products, arithmetic and copies ran while one was open for 0% of the time, Pallas kernels for 5%

profile of v3, /device:TPU:0, one launch (start us, length us, event | category | flops | bytes accessed | tf_op | source)
XLA Modules:
  0.0 50.7 jit_solution(14703020109818691)
XLA Ops:
  0.6 1.0 %copy-done = bf16[256,768]{1,0:T(8,128)(2,1)S(1)} copy-done((bf16[256,768]{1,0:T(8,128)(2,1)S(1)}, bf16[256,768]{1,0:T(8,128)(2,1)}, u32[]{:S(2)}) %copy-start) | copy-done | bytes 393240
  1.6 0.7 %copy-done.1 = s32[256]{0:T(256)S(1)} copy-done((s32[256]{0:T(256)S(1)}, s32[256]{0:T(256)}, u32[]{:S(2)}) %copy-start.1) | copy-done | bytes 1048
  2.3 0.4 sort_rows.1
  2.7 3.0 %collective-permute-start.6 = (bf16[64,768]{1,0:T(8,128)(2,1)S(1)}, bf16[64,768]{1,0:T(8,128)(2,1)S(1)}, u32[]{:S(2)}, u32[]{:S(2)}) collective-permute-start(bf16[64,768]{1,0:T(8,128)(2,1)S(1)} %get-tuple-element.19), channel_id=1, source_target_pairs={{0,2},{1,5},{2,0},{3,7},{4,6},{5,1},{6,4},{7,3},{8,10},{9,13},{10,... | collective-permute-start | bytes 294920 | tf_op jit(solution)/shard_map/ppermute | solution.py:176
  5.7 1.6 %collective-permute-start = (bf16[64,768]{1,0:T(8,128)(2,1)S(1)}, bf16[64,768]{1,0:T(8,128)(2,1)S(1)}, u32[]{:S(2)}, u32[]{:S(2)}) collective-permute-start(bf16[64,768]{1,0:T(8,128)(2,1)S(1)} %get-tuple-element.20), channel_id=1, source_target_pairs={{0,8},{8,0},{16,24},{24,16},{1,9},{9,1},{17,25},{25,17},{2,10},{10... | collective-permute-start | bytes 294920 | tf_op jit(solution)/shard_map/ppermute | solution.py:170
  7.3 2.6 %collective-permute-start.1 = (bf16[64,768]{1,0:T(8,128)(2,1)S(1)}, bf16[64,768]{1,0:T(8,128)(2,1)S(1)}, u32[]{:S(2)}, u32[]{:S(2)}) collective-permute-start(bf16[64,768]{1,0:T(8,128)(2,1)S(1)} %get-tuple-element.21), channel_id=1, source_target_pairs={{0,16},{8,24},{16,0},{24,8},{1,17},{9,25},{17,1},{25,9},{2,18},{10... | collective-permute-start | bytes 294920 | tf_op jit(solution)/shard_map/ppermute | solution.py:170
  9.9 0.2 collective-permute-start.2
  10.1 0.0 collective-permute-done.6
  10.2 1.6 %collective-permute-start.7 = (bf16[128,768]{1,0:T(8,128)(2,1)S(1)}, bf16[128,768]{1,0:T(8,128)(2,1)S(1)}, u32[]{:S(2)}, u32[]{:S(2)}) collective-permute-start(bf16[128,768]{1,0:T(8,128)(2,1)S(1)} %pad_maximum_fusion.3), channel_id=1, source_target_pairs={{0,4},{1,3},{2,6},{3,1},{4,0},{5,7},{6,2},{7,5},{8,12},{9,11},{10,... | collective-permute-start | bytes 589832 | tf_op jit(solution)/shard_map/ppermute | solution.py:176
  11.7 0.0 collective-permute-done
  11.7 0.5 %collective-permute-start.3 = (bf16[64,768]{1,0:T(8,128)(2,1)S(1)}, bf16[64,768]{1,0:T(8,128)(2,1)S(1)}, u32[]{:S(2)}, u32[]{:S(2)}) collective-permute-start(bf16[64,768]{1,0:T(8,128)(2,1)S(1)} %collective-permute-done), channel_id=1, source_target_pairs={{0,2},{1,5},{2,0},{3,7},{4,6},{5,1},{6,4},{7,3},{8,10},{9,13},{10,... | collective-permute-start | bytes 294920 | tf_op jit(solution)/shard_map/ppermute | solution.py:176
  12.3 4.1 %collective-permute-done.3 = bf16[64,768]{1,0:T(8,128)(2,1)S(1)} collective-permute-done((bf16[64,768]{1,0:T(8,128)(2,1)S(1)}, bf16[64,768]{1,0:T(8,128)(2,1)S(1)}, u32[]{:S(2)}, u32[]{:S(2)}) %collective-permute-start.3) | collective-permute-done | bytes 98336 | tf_op jit(solution)/shard_map/ppermute | solution.py:176
  16.4 1.1 %collective-permute-done.1 = bf16[64,768]{1,0:T(8,128)(2,1)S(1)} collective-permute-done((bf16[64,768]{1,0:T(8,128)(2,1)S(1)}, bf16[64,768]{1,0:T(8,128)(2,1)S(1)}, u32[]{:S(2)}, u32[]{:S(2)}) %collective-permute-start.1) | collective-permute-done | bytes 98336 | tf_op jit(solution)/shard_map/ppermute | solution.py:170
  17.5 0.0 collective-permute-done.2
  17.5 0.5 collective-permute-start.8
  18.0 1.6 %collective-permute-start.4 = (bf16[128,768]{1,0:T(8,128)(2,1)S(1)}, bf16[128,768]{1,0:T(8,128)(2,1)S(1)}, u32[]{:S(2)}, u32[]{:S(2)}) collective-permute-start(bf16[128,768]{1,0:T(8,128)(2,1)S(1)} %pad_maximum_fusion.2), channel_id=1, source_target_pairs={{0,2},{1,5},{2,0},{3,7},{4,6},{5,1},{6,4},{7,3},{8,10},{9,13},{10,... | collective-permute-start | bytes 589832 | tf_op jit(solution)/shard_map/ppermute | solution.py:176
  19.6 0.0 collective-permute-done.7
  19.6 4.6 %collective-permute-done.8 = bf16[128,768]{1,0:T(8,128)(2,1)S(1)} collective-permute-done((bf16[128,768]{1,0:T(8,128)(2,1)S(1)}, bf16[128,768]{1,0:T(8,128)(2,1)S(1)}, u32[]{:S(2)}, u32[]{:S(2)}) %collective-permute-start.8) | collective-permute-done | bytes 196640 | tf_op jit(solution)/shard_map/ppermute | solution.py:176
  24.2 0.1 collective-permute-start.9
  24.4 1.1 %collective-permute-start.5 = (bf16[256,768]{1,0:T(8,128)(2,1)S(1)}, bf16[256,768]{1,0:T(8,128)(2,1)S(1)}, u32[]{:S(2)}, u32[]{:S(2)}) collective-permute-start(bf16[256,768]{1,0:T(8,128)(2,1)S(1)} %pad_maximum_fusion), channel_id=1, source_target_pairs={{0,4},{1,3},{2,6},{3,1},{4,0},{5,7},{6,2},{7,5},{8,12},{9,11},{10,... | collective-permute-start | bytes 1179656 | tf_op jit(solution)/shard_map/ppermute | solution.py:176
  25.5 1.7 %collective-permute-done.9.refs_1_ = bf16[768,768]{1,0:T(8,128)(2,1)S(1)} collective-permute-done((bf16[768,768]{1,0:T(8,128)(2,1)S(1)}, bf16[768,768]{1,0:T(8,128)(2,1)S(1)}, u32[]{:S(2)}, u32[]{:S(2)}) %collective-permute-start.9) | collective-permute-done | bytes 1179680 | tf_op jit(solution)/shard_map/ppermute | solution.py:179
  27.1 2.3 %early_sums.1 = (f32[256,768]{1,0:T(8,128)S(1)}, f32[256,128]{1,0:T(8,128)S(1)}) custom-call(bf16[256,768]{1,0:T(8,128)(2,1)S(1)} %constant_dynamic-update-slice_fusion.rows_ref, bf16[768,768]{1,0:T(8,128)(2,1)S(1)} %constant_dynamic-update-slice_fusion.4.refs_0_, bf16[768,768]{1,0:T(8,128)(2,1)S(1)} %collective-permute-done.9.refs_1_), custom_call_target="tpu_custom_call" | custom-call | flops 1207959552 | tf_op jit(solution)/shard_map/early_sums/pallas_call | solution.py:209
  29.5 2.7 %collective-permute-done.5.refs_0_ = bf16[256,768]{1,0:T(8,128)(2,1)S(1)} collective-permute-done((bf16[256,768]{1,0:T(8,128)(2,1)S(1)}, bf16[256,768]{1,0:T(8,128)(2,1)S(1)}, u32[]{:S(2)}, u32[]{:S(2)}) %collective-permute-start.5) | collective-permute-done | bytes 393248 | tf_op jit(solution)/shard_map/ppermute | solution.py:176
  32.2 1.7 %collective-permute-done.10.refs_1_ = bf16[256,768]{1,0:T(8,128)(2,1)S(1)} collective-permute-done((bf16[256,768]{1,0:T(8,128)(2,1)S(1)}, bf16[256,768]{1,0:T(8,128)(2,1)S(1)}, u32[]{:S(2)}, u32[]{:S(2)}) %collective-permute-start.10) | collective-permute-done | bytes 393248 | tf_op jit(solution)/shard_map/ppermute | solution.py:179
  33.9 1.1 %last_sums.1 = (f32[72,768]{1,0:T(8,128)S(1)}, f32[72,768]{1,0:T(8,128)S(1)}, f32[72,768]{1,0:T(8,128)S(1)}, f32[72,768]{1,0:T(8,128)S(1)}) custom-call(bf16[256,768]{1,0:T(8,128)(2,1)S(1)} %constant_dynamic-update-slice_fusion.rows_ref, f32[256,768]{1,0:T(8,128)S(1)} %get-tuple-element.27.total_ref, f32[256,128]{1,0:T(8,128)S(1)} %get-tuple-element.28.dens_ref, ...), custom_call_target="tpu_custom_call" | custom-call | flops 402653184 | tf_op jit(solution)/shard_map/last_sums/pallas_call | solution.py:223
  35.1 0.0 copy-start.2
  35.1 2.5 %collective-permute-start.11 = (f16[72,768]{1,0:T(8,128)(2,1)S(1)}, f16[72,768]{1,0:T(8,128)(2,1)S(1)}, u32[]{:S(2)}, u32[]{:S(2)}) collective-permute-start(f16[72,768]{1,0:T(8,128)(2,1)S(1)} %convert_element_type.26), channel_id=1, source_target_pairs={{0,8},{8,0},{16,24},{24,16},{1,9},{9,1},{17,25},{25,17},{2,10},{10... | collective-permute-start | bytes 331784 | tf_op jit(solution)/shard_map/ppermute | solution.py:170
  37.7 1.4 %collective-permute-start.12 = (f16[72,768]{1,0:T(8,128)(2,1)S(1)}, f16[72,768]{1,0:T(8,128)(2,1)S(1)}, u32[]{:S(2)}, u32[]{:S(2)}) collective-permute-start(f16[72,768]{1,0:T(8,128)(2,1)S(1)} %convert_element_type.28), channel_id=1, source_target_pairs={{0,16},{8,24},{16,0},{24,8},{1,17},{9,25},{17,1},{25,9},{2,18},{10... | collective-permute-start | bytes 331784 | tf_op jit(solution)/shard_map/ppermute | solution.py:170
  39.1 1.3 %collective-permute-start.13 = (f16[72,768]{1,0:T(8,128)(2,1)S(1)}, f16[72,768]{1,0:T(8,128)(2,1)S(1)}, u32[]{:S(2)}, u32[]{:S(2)}) collective-permute-start(f16[72,768]{1,0:T(8,128)(2,1)S(1)} %convert_element_type.30), channel_id=1, source_target_pairs={{0,24},{8,16},{16,8},{24,0},{1,25},{9,17},{17,9},{25,1},{2,26},{10... | collective-permute-start | bytes 331784 | tf_op jit(solution)/shard_map/ppermute | solution.py:170
  40.4 0.7 %collective-permute-done.11 = f16[72,768]{1,0:T(8,128)(2,1)S(1)} collective-permute-done((f16[72,768]{1,0:T(8,128)(2,1)S(1)}, f16[72,768]{1,0:T(8,128)(2,1)S(1)}, u32[]{:S(2)}, u32[]{:S(2)}) %collective-permute-start.11) | collective-permute-done | bytes 110624 | tf_op jit(solution)/shard_map/ppermute | solution.py:170
  41.1 8.1 %collective-permute-done.12 = f16[72,768]{1,0:T(8,128)(2,1)S(1)} collective-permute-done((f16[72,768]{1,0:T(8,128)(2,1)S(1)}, f16[72,768]{1,0:T(8,128)(2,1)S(1)}, u32[]{:S(2)}, u32[]{:S(2)}) %collective-permute-start.12) | collective-permute-done | bytes 110624 | tf_op jit(solution)/shard_map/ppermute | solution.py:170
  49.2 1.5 %restore_rows.1 = (f32[256,768]{1,0:T(8,128)}, f32[1,256]{1,0:T(1,128)}) custom-call(s32[1]{0:T(128)} %bitcast.own_ref, s32[1,256]{1,0:T(1,128)S(1)} %bitcast.4, f32[72,768]{1,0:T(8,128)S(1)} %convert_convert_fusion.refs_0_, f32[72,768]{1,0:T(8,128)S(1)} %convert_element_type.27.refs_1_, f32[72,768]{1,0:T(8,128)S(1)} %convert_element_type.29.refs_2_, ...), custom_call_target="tpu_custom_call" | custom-call | tf_op jit(solution)/shard_map/restore_rows/pallas_call | solution.py:239
  (28 shorter events, 0.3 us)
Async XLA Ops:
  0.6 1.0 %copy-start = (bf16[256,768]{1,0:T(8,128)(2,1)S(1)}, bf16[256,768]{1,0:T(8,128)(2,1)}, u32[]{:S(2)}) copy-start(bf16[256,768]{1,0:T(8,128)(2,1)} %rows_ref.1) | copy-start | bytes 1179652
  1.6 0.7 %copy-start.1 = (s32[256]{0:T(256)S(1)}, s32[256]{0:T(256)}, u32[]{:S(2)}) copy-start(s32[256]{0:T(256)} %param.3) | copy-start | bytes 3076
  2.7 7.4 %collective-permute-start.6 = (bf16[64,768]{1,0:T(8,128)(2,1)S(1)}, bf16[64,768]{1,0:T(8,128)(2,1)S(1)}, u32[]{:S(2)}, u32[]{:S(2)}) collective-permute-start(bf16[64,768]{1,0:T(8,128)(2,1)S(1)} %get-tuple-element.19), channel_id=1, source_target_pairs={{0,2},{1,5},{2,0},{3,7},{4,6},{5,1},{6,4},{7,3},{8,10},{9,13},{10,... | collective-permute-start | bytes 294920 | tf_op jit(solution)/shard_map/ppermute | solution.py:176
  5.7 6.0 %collective-permute-start = (bf16[64,768]{1,0:T(8,128)(2,1)S(1)}, bf16[64,768]{1,0:T(8,128)(2,1)S(1)}, u32[]{:S(2)}, u32[]{:S(2)}) collective-permute-start(bf16[64,768]{1,0:T(8,128)(2,1)S(1)} %get-tuple-element.20), channel_id=1, source_target_pairs={{0,8},{8,0},{16,24},{24,16},{1,9},{9,1},{17,25},{25,17},{2,10},{10... | collective-permute-start | bytes 294920 | tf_op jit(solution)/shard_map/ppermute | solution.py:170
  7.3 10.2 %collective-permute-start.1 = (bf16[64,768]{1,0:T(8,128)(2,1)S(1)}, bf16[64,768]{1,0:T(8,128)(2,1)S(1)}, u32[]{:S(2)}, u32[]{:S(2)}) collective-permute-start(bf16[64,768]{1,0:T(8,128)(2,1)S(1)} %get-tuple-element.21), channel_id=1, source_target_pairs={{0,16},{8,24},{16,0},{24,8},{1,17},{9,25},{17,1},{25,9},{2,18},{10... | collective-permute-start | bytes 294920 | tf_op jit(solution)/shard_map/ppermute | solution.py:170
  9.9 7.6 %collective-permute-start.2 = (bf16[64,768]{1,0:T(8,128)(2,1)S(1)}, bf16[64,768]{1,0:T(8,128)(2,1)S(1)}, u32[]{:S(2)}, u32[]{:S(2)}) collective-permute-start(bf16[64,768]{1,0:T(8,128)(2,1)S(1)} %get-tuple-element.22), channel_id=1, source_target_pairs={{0,24},{8,16},{16,8},{24,0},{1,25},{9,17},{17,9},{25,1},{2,26},{10... | collective-permute-start | bytes 294920 | tf_op jit(solution)/shard_map/ppermute | solution.py:170
  10.2 9.4 %collective-permute-start.7 = (bf16[128,768]{1,0:T(8,128)(2,1)S(1)}, bf16[128,768]{1,0:T(8,128)(2,1)S(1)}, u32[]{:S(2)}, u32[]{:S(2)}) collective-permute-start(bf16[128,768]{1,0:T(8,128)(2,1)S(1)} %pad_maximum_fusion.3), channel_id=1, source_target_pairs={{0,4},{1,3},{2,6},{3,1},{4,0},{5,7},{6,2},{7,5},{8,12},{9,11},{10,... | collective-permute-start | bytes 589832 | tf_op jit(solution)/shard_map/ppermute | solution.py:176
  11.7 4.6 %collective-permute-start.3 = (bf16[64,768]{1,0:T(8,128)(2,1)S(1)}, bf16[64,768]{1,0:T(8,128)(2,1)S(1)}, u32[]{:S(2)}, u32[]{:S(2)}) collective-permute-start(bf16[64,768]{1,0:T(8,128)(2,1)S(1)} %collective-permute-done), channel_id=1, source_target_pairs={{0,2},{1,5},{2,0},{3,7},{4,6},{5,1},{6,4},{7,3},{8,10},{9,13},{10,... | collective-permute-start | bytes 294920 | tf_op jit(solution)/shard_map/ppermute | solution.py:176
  17.5 6.7 %collective-permute-start.8 = (bf16[128,768]{1,0:T(8,128)(2,1)S(1)}, bf16[128,768]{1,0:T(8,128)(2,1)S(1)}, u32[]{:S(2)}, u32[]{:S(2)}) collective-permute-start(bf16[128,768]{1,0:T(8,128)(2,1)S(1)} %pad_maximum_fusion.1), channel_id=1, source_target_pairs={{0,4},{1,3},{2,6},{3,1},{4,0},{5,7},{6,2},{7,5},{8,12},{9,11},{10,... | collective-permute-start | bytes 589832 | tf_op jit(solution)/shard_map/ppermute | solution.py:176
  18.0 6.2 %collective-permute-start.4 = (bf16[128,768]{1,0:T(8,128)(2,1)S(1)}, bf16[128,768]{1,0:T(8,128)(2,1)S(1)}, u32[]{:S(2)}, u32[]{:S(2)}) collective-permute-start(bf16[128,768]{1,0:T(8,128)(2,1)S(1)} %pad_maximum_fusion.2), channel_id=1, source_target_pairs={{0,2},{1,5},{2,0},{3,7},{4,6},{5,1},{6,4},{7,3},{8,10},{9,13},{10,... | collective-permute-start | bytes 589832 | tf_op jit(solution)/shard_map/ppermute | solution.py:176
  24.2 2.9 %collective-permute-start.9 = (bf16[768,768]{1,0:T(8,128)(2,1)S(1)}, bf16[768,768]{1,0:T(8,128)(2,1)S(1)}, u32[]{:S(2)}, u32[]{:S(2)}) collective-permute-start(bf16[768,768]{1,0:T(8,128)(2,1)S(1)} %constant_dynamic-update-slice_fusion.4.refs_0_), channel_id=1, source_target_pairs={{0,1},{1,0},{2,3},{3,2},{4,5},{5,4},{6,7},{7,6},{8,9},{9,8},{10,11... | collective-permute-start | bytes 3538952 | tf_op jit(solution)/shard_map/ppermute | solution.py:179
  24.4 7.8 %collective-permute-start.5 = (bf16[256,768]{1,0:T(8,128)(2,1)S(1)}, bf16[256,768]{1,0:T(8,128)(2,1)S(1)}, u32[]{:S(2)}, u32[]{:S(2)}) collective-permute-start(bf16[256,768]{1,0:T(8,128)(2,1)S(1)} %pad_maximum_fusion), channel_id=1, source_target_pairs={{0,4},{1,3},{2,6},{3,1},{4,0},{5,7},{6,2},{7,5},{8,12},{9,11},{10,... | collective-permute-start | bytes 1179656 | tf_op jit(solution)/shard_map/ppermute | solution.py:176
  32.2 1.7 %collective-permute-start.10 = (bf16[256,768]{1,0:T(8,128)(2,1)S(1)}, bf16[256,768]{1,0:T(8,128)(2,1)S(1)}, u32[]{:S(2)}, u32[]{:S(2)}) collective-permute-start(bf16[256,768]{1,0:T(8,128)(2,1)S(1)} %collective-permute-done.5.refs_0_), channel_id=1, source_target_pairs={{0,1},{1,0},{2,3},{3,2},{4,5},{5,4},{6,7},{7,6},{8,9},{9,8},{10,11... | collective-permute-start | bytes 1179656 | tf_op jit(solution)/shard_map/ppermute | solution.py:179
  35.1 14.2 %copy-start.2 = (s32[256]{0:T(256)S(1)}, s32[256]{0:T(256)}, u32[]{:S(2)}) copy-start(s32[256]{0:T(256)} %param.3) | copy-start | bytes 3076
  35.1 6.0 %collective-permute-start.11 = (f16[72,768]{1,0:T(8,128)(2,1)S(1)}, f16[72,768]{1,0:T(8,128)(2,1)S(1)}, u32[]{:S(2)}, u32[]{:S(2)}) collective-permute-start(f16[72,768]{1,0:T(8,128)(2,1)S(1)} %convert_element_type.26), channel_id=1, source_target_pairs={{0,8},{8,0},{16,24},{24,16},{1,9},{9,1},{17,25},{25,17},{2,10},{10... | collective-permute-start | bytes 331784 | tf_op jit(solution)/shard_map/ppermute | solution.py:170
  37.7 11.5 %collective-permute-start.12 = (f16[72,768]{1,0:T(8,128)(2,1)S(1)}, f16[72,768]{1,0:T(8,128)(2,1)S(1)}, u32[]{:S(2)}, u32[]{:S(2)}) collective-permute-start(f16[72,768]{1,0:T(8,128)(2,1)S(1)} %convert_element_type.28), channel_id=1, source_target_pairs={{0,16},{8,24},{16,0},{24,8},{1,17},{9,25},{17,1},{25,9},{2,18},{10... | collective-permute-start | bytes 331784 | tf_op jit(solution)/shard_map/ppermute | solution.py:170
  39.1 10.1 %collective-permute-start.13 = (f16[72,768]{1,0:T(8,128)(2,1)S(1)}, f16[72,768]{1,0:T(8,128)(2,1)S(1)}, u32[]{:S(2)}, u32[]{:S(2)}) collective-permute-start(f16[72,768]{1,0:T(8,128)(2,1)S(1)} %convert_element_type.30), channel_id=1, source_target_pairs={{0,24},{8,16},{16,8},{24,0},{1,25},{9,17},{17,9},{25,1},{2,26},{10... | collective-permute-start | bytes 331784 | tf_op jit(solution)/shard_map/ppermute | solution.py:170
